TPU v7x, 32 devices: a whole 2x2x4 slice. The times are simulated.
32 devices in a mesh: dp: 4 (over z), expert: 8 (over y, x, core).
Axes of the slice: x: 2, y: 2, z: 4, core: 2. Of those that a mesh axis runs over, the one named last changes fastest.
Arguments:
- route_ids: int32 [4096, 8], P(('dp', 'expert')), may hold values from 0 to 127, all different within a row; in each aligned block of 128 rows (0 to 127, 128 to 255, ...) at most 16 rows name the same one
- route_probs: float32 [4096, 8], P(('dp', 'expert')), may hold values from 0.05 to 0.6
- capacity: int32 [8], replicated, may hold values from 4 to 16, as said below
- hot_lists: int32 [4, 4], P('dp'), may hold values from 0 to 7, as said below
- gate_up: bfloat16 [4, 8, 128, 1536], P('dp', 'expert'), may hold values from -6 to 6
- w_quant: bfloat16 [8, 768, 4096], P('expert'), may hold values from -0.21875 to 0.21875
- w_scale: float32 [8, 6, 32], P('expert'), may hold values from 0.5 to 2
- d_out: bfloat16 [4096, 4096], P(('dp', 'expert')), may hold values from -6 to 6
Outputs:
- combined: bfloat16 [4096, 4096], P(('dp', 'expert'))
- d_probs: float32 [4096, 8], P(('dp', 'expert'))
- d_gate_up: bfloat16 [4, 8, 128, 1536], P('dp', 'expert')
- d_w_down: bfloat16 [8, 4096, 768], P('expert', 'dp')
Inputs may be any that keep to these rules, and one draw needn't show every extreme that they name: `route_ids`: each row names 8 different experts; among the rows of one device no expert is named more than 16 times, a bound that some block reaches. `capacity`: each entry is a multiple of 4; some expert has exactly 16. `hot_lists`: each row names 4 different experts among the 8 computed ones.
All inputs are finite; a program needn't handle non-finite values.
Results may differ from a plain program's by a relative error of at most 0.017.
Values may be sent and summed in bfloat16 or wider, within the bound.
No kernel may reach another device: no remote copies, remote signals or barrier semaphores. Data moves between devices by JAX's collectives and lax.ppermute only.
A program may use at most 128 MiB of HBM per device.

v0:
```python
import jax
import jax.numpy as jnp
from jax import lax
from jax.sharding import PartitionSpec as P

D = 4096
TOPK = 8
HID = 768
QB = 128
CAP = 16


def routing(expert_ids, capacity, hot_row, flight):
    experts_iota = jnp.arange(flight, dtype=jnp.int32)
    onehot = (expert_ids[:, None] == experts_iota[None, :]).astype(jnp.int32)
    earlier = jnp.cumsum(onehot, axis=0) - onehot
    slot_rank = jnp.sum(earlier * onehot, axis=1)
    hot_count = jnp.sum((hot_row[:, None] == experts_iota[None, :]).astype(jnp.int32), axis=0)
    limits = jnp.where(hot_count > 0, CAP, capacity)
    row_limit = jnp.sum(onehot * limits[None, :], axis=1)
    kept_mask = (expert_ids < flight) & (slot_rank < row_limit)
    return (kept_mask, slot_rank)


def dequant(quantized, block_scale):
    expanded = jnp.repeat(jnp.repeat(block_scale, QB, axis=0), QB, axis=1)
    return (quantized.astype(jnp.float32) * expanded).astype(jnp.bfloat16)


def swiglu_parts(arrived):
    gate_in = arrived[..., :HID].astype(jnp.float32)
    up_in = arrived[..., HID:].astype(jnp.float32)
    return (gate_in, up_in, jax.nn.sigmoid(gate_in))


def shards(route_ids, route_probs, capacity, hot_lists, gate_up, w_quant, w_scale, d_out):
    flight = lax.axis_size("expert")
    slot_count = flight * CAP
    tokens_here = route_ids.shape[0]
    expert_ids = route_ids.reshape(-1)
    kept_mask, slot_rank = routing(expert_ids, capacity, hot_lists[0], flight)
    slot_index = jnp.where(kept_mask, expert_ids * CAP + slot_rank, flight * CAP)
    route_weight = jnp.where(kept_mask, route_probs.reshape(-1), 0.0).reshape(tokens_here, TOPK)
    weight = dequant(w_quant[0], w_scale[0])
    gate_in, up_in, sig_gate = swiglu_parts(gate_up[0, 0])
    silu_gate = gate_in * sig_gate
    hidden = (silu_gate * up_in).astype(jnp.bfloat16)
    expert_out = jnp.dot(hidden, weight, preferred_element_type=jnp.float32).astype(jnp.bfloat16)
    returned = lax.all_to_all(
        expert_out.reshape(flight, CAP, D), "expert", split_axis=0, concat_axis=0, tiled=True
    )
    padded = jnp.concatenate(
        [returned.reshape(flight * CAP, D), jnp.zeros((1, D), jnp.bfloat16)], axis=0
    )
    picked = padded[slot_index].reshape(tokens_here, TOPK, D)
    combined = jnp.einsum(
        "tkd,tk->td", picked, route_weight, preferred_element_type=jnp.float32
    ).astype(jnp.bfloat16)
    d_probs = jnp.einsum("tkd,td->tk", picked, d_out, preferred_element_type=jnp.float32)
    cotangent = d_out.astype(jnp.float32)
    sent_rows = (
        (route_weight[:, :, None] * cotangent[:, None, :])
        .astype(jnp.bfloat16)
        .reshape(tokens_here * TOPK, D)
    )
    outgoing = (
        jnp.zeros((flight * CAP + 1, D), jnp.bfloat16).at[slot_index].set(sent_rows)[: flight * CAP]
    )
    arrived_grads = lax.all_to_all(
        outgoing.reshape(flight, CAP, D), "expert", split_axis=0, concat_axis=0, tiled=True
    ).reshape(slot_count, D)
    d_hidden = jnp.einsum("sd,hd->sh", arrived_grads, weight, preferred_element_type=jnp.float32)
    d_gate = d_hidden * up_in * sig_gate * (1.0 + gate_in * (1.0 - sig_gate))
    d_up = d_hidden * silu_gate
    d_gate_up = jnp.concatenate([d_gate, d_up], axis=1).astype(jnp.bfloat16)
    term = jnp.einsum("sd,sh->dh", arrived_grads, hidden, preferred_element_type=jnp.float32)
    d_weight = lax.psum_scatter(
        lax.optimization_barrier(term.astype(jnp.bfloat16))
        .astype(jnp.float32)
        .astype(jnp.bfloat16),
        "dp",
        scatter_dimension=0,
        tiled=True,
    )
    return (combined, d_probs, d_gate_up[None, None], d_weight[None])


def solution(mesh):
    placed = (
        P(("dp", "expert"), None),
        P(("dp", "expert"), None),
        P(),
        P("dp", None),
        P("dp", "expert", None, None),
        P("expert", None, None),
        P("expert", None, None),
        P(("dp", "expert"), None),
    )
    return jax.shard_map(
        shards,
        mesh=mesh,
        in_specs=placed,
        out_specs=(
            P(("dp", "expert"), None),
            P(("dp", "expert"), None),
            P("dp", "expert", None, None),
            P("expert", "dp", None),
        ),
        check_vma=False,
    )
```

profile of v0, /device:TPU:0, one launch (start us, length us, event | category | flops | bytes accessed | tf_op | source)
XLA Modules:
  0.0 171.2 jit_solution(17086310901875599900)
XLA Ops:
  7.2 0.8 copy.17
  8.2 0.7 broadcast_multiply_fusion
  8.9 2.3 %reduce-window.6 = s32[8,8,128]{2,1,0:T(8,128)S(1)} reduce-window(s32[8,8,128]{2,1,0:T(8,128)S(1)} %fusion.35, s32[]{:T(128)} %constant.11.clone.1), window={size=1x1x128 pad=0_0x0_0x127_0}, to_apply=%region_0.0 | reduce-window | flops 1040384 | bytes 65540 | tf_op jit(solution)/shard_map/reduce-window
  11.7 0.8 convert_reduce_fusion
  13.3 0.8 copy.21
  14.8 1.4 convert_element_type.88
  16.3 11.8 %scatter_custom_fusion = bf16[129,4096]{1,0:T(8,128)(2,1)S(1)} fusion(s32[1024]{0:T(1024)S(1)} %bitcast.106, f32[128,4096]{1,0:T(8,128)S(1)} %convert_element_type.88, f32[1024]{0:T(1024)S(1)} %mul.87, bf16[]{:T(256)} %constant.9.clone.1), kind=kCustom, calls=%fused_computation.10 | custom fusion | flops 8388608 | bytes 3158018 | tf_op jit(solution)/shard_map/scatter | solution.py:67
  28.1 20.3 %all_to_all.10 = bf16[8,16,4096]{2,1,0:T(8,128)(2,1)S(1)} all-to-all(bf16[8,16,4096]{2,1,0:T(8,128)(2,1)S(1)} %bitcast.94), channel_id=1, replica_groups=mesh['dp'=4,'expert'=8] {'expert'}, dimensions={0} | all-to-all | bytes 2097152 | tf_op jit(solution)/shard_map/all_to_all | solution.py:69
  48.5 5.6 %convolution_convert_fusion = bf16[4096,768]{1,0:T(8,128)(2,1)} fusion(bf16[128,4096]{1,0:T(8,128)(2,1)S(1)} %bitcast.89, bf16[128,1536]{1,0:T(8,128)(2,1)} %bitcast.100), kind=kOutput, calls=%fused_computation.17 | convolution fusion | flops 809238528 | bytes 7733248 | tf_op jit(solution)/shard_map/sd,sh->dh/dot_general | solution.py:76
  54.2 3.5 %broadcast_in_dim.33 = f32[768,32,128]{2,1,0:T(8,128)S(1)} broadcast(f32[768,32]{1,0:T(8,128)S(1)} %bitcast.95), dimensions={0,1} | broadcast | bytes 12681216 | tf_op jit(solution)/shard_map/broadcast_in_dim | solution.py:26
  57.7 8.6 %fusion.17 = bf16[128,4096]{1,0:T(8,128)(2,1)} fusion(bf16[1,768,4096]{2,1,0:T(8,128)(2,1)S(1)} %bitcast.88, f32[96,8,32,128]{3,2,1,0:T(8,128)S(1)} %bitcast.86, bf16[128,1536]{1,0:T(8,128)(2,1)S(1)} %bitcast.101), kind=kOutput, calls=%fused_computation.22 | convolution fusion | flops 816054272 | bytes 20316160 | tf_op jit(solution)/shard_map/dot_general | solution.py:48
  66.2 3.8 %all-to-all-start = ((bf16[8,16,4096]{2,1,0:T(8,128)(2,1)}), bf16[8,16,4096]{2,1,0:T(8,128)(2,1)S(1)}, u32[]{:S(2)}, u32[]{:S(2)}) async-start(bf16[8,16,4096]{2,1,0:T(8,128)(2,1)} %bitcast.92), calls=%async_computation | async-start | bytes 2097152 | tf_op jit(solution)/shard_map/all_to_all | solution.py:49
  70.0 9.1 %convert_bitcast_fusion = f32[96,8,32,128]{3,1,2,0:T(8,128)} fusion(bf16[1,768,4096]{2,1,0:T(8,128)(2,1)} %param.13), kind=kLoop, calls=%fused_computation.4 | loop fusion | flops 3145728 | bytes 18874368
  79.1 12.2 %copy.29 = f32[96,8,32,128]{3,2,1,0:T(8,128)} copy(f32[96,8,32,128]{3,1,2,0:T(8,128)} %convert_bitcast_fusion) | data formatting | bytes 25165824
  91.3 10.9 %fusion.3 = bf16[768,32,128]{2,1,0:T(8,128)(2,1)} fusion(f32[96,8,32,128]{3,2,1,0:T(8,128)} %copy.29, f32[768,32]{1,0:T(8,128)S(1)} %bitcast.96), kind=kLoop, calls=%fused_computation.9 | loop fusion | flops 6291456 | bytes 18972672 | tf_op jit(solution)/shard_map/convert_element_type | solution.py:27
  102.2 1.0 copy-done
  103.2 1.3 concatenate.18
  104.6 7.7 %gather_fusion = bf16[1024,4096]{1,0:T(8,128)(2,1)} fusion(bf16[129,4096]{1,0:T(8,128)(2,1)S(1)} %concatenate.18, s32[1024]{0:T(1024)S(1)} %broadcast_clamp_fusion), kind=kCustom, calls=%fused_computation | custom fusion | bytes 16781312 | tf_op jit(solution)/shard_map/gather | solution.py:55
  112.3 5.7 %fusion.8 = bf16[128,1,4096]{2,1,0:T(2,128)(2,1)S(1)} fusion(f32[128,8,1]{1,2,0:T(1,128)S(1)} %bitcast.99, bf16[1024,4096]{1,0:T(8,128)(2,1)} %gather_fusion), kind=kOutput, calls=%fused_computation.13 | convolution fusion | flops 8388608 | bytes 9441280 | tf_op jit(solution)/shard_map/tkd,tk->td/dot_general | solution.py:56
  118.0 2.1 %copy.46 = bf16[128,1,4096]{2,0,1:T(8,128)(2,1)} copy(bf16[128,1,4096]{2,1,0:T(2,128)(2,1)S(1)} %fusion.8) | data formatting | bytes 2097152 | tf_op jit(solution)/shard_map/tkd,tk->td/dot_general | solution.py:56
  120.1 9.1 %fusion.6 = f32[128,1,8]{2,1,0:T(1,128)S(1)} fusion(bf16[1024,4096]{1,0:T(8,128)(2,1)} %gather_fusion, bf16[128,4096,1]{1,0,2:T(8,128)(2,1)} %bitcast.97), kind=kOutput, calls=%fused_computation.11 | convolution fusion | flops 8388608 | bytes 9441280 | tf_op jit(solution)/shard_map/tkd,td->tk/dot_general | solution.py:59
  129.9 6.0 %fusion.31 = (bf16[1,1,128,768]{3,2,1,0:T(8,128)(2,1)S(1)}, bf16[1,1,128,768]{3,2,1,0:T(8,128)(2,1)S(1)}) fusion(bf16[128,1536]{1,0:T(8,128)(2,1)S(1)} %bitcast.102, bf16[128,4096]{1,0:T(8,128)(2,1)S(1)} %bitcast.90, bf16[96,8,32,128]{3,2,1,0:T(8,128)(2,1)} %bitcast.91), kind=kOutput, calls=%fused_computation.42 | convolution fusion | flops 806780928 | bytes 8126464 | tf_op jit(solution)/shard_map/sd,hd->sh/dot_general | solution.py:72
  135.9 0.8 pad_maximum_fusion
  136.7 27.7 %reduce-scatter.2.cloned.1.call-done = bf16[1024,768]{1,0:T(8,128)(2,1)} async-done(((bf16[4096,768]{1,0:T(8,128)(2,1)}), bf16[1024,768]{1,0:T(8,128)(2,1)}) %reduce-scatter.2.cloned.1.call-update) | async-done | bytes 1572880 | tf_op jit(solution)/shard_map/reduce_scatter | solution.py:77
  (40 shorter events, 3.2 us)
Async XLA Ops:
  7.2 157.2 %reduce-scatter.2.cloned.1.call-start = ((), (), s32[]{:S(2)}) async-start(), calls=%async_computation.3 | async-start | bytes 7864320 | tf_op jit(solution)/shard_map/reduce_scatter | solution.py:77
  14.1 0.6 copy-start.1
  48.4 5.6 %copy-start.5 = (f32[1,6,32]{2,0,1:T(1,128)S(1)}, f32[1,6,32]{2,0,1:T(1,128)}, u32[]{:S(2)}) copy-start(f32[1,6,32]{2,0,1:T(1,128)} %param.14) | copy-start | bytes 2308
  54.0 3.6 %slice-start = ((s8[6291456]{0:T(1024)(128)(4,1)}), s8[2097152]{0:T(1024)(128)(4,1)S(1)}, s32[]{:S(2)}) async-start(s8[6291456]{0:T(1024)(128)(4,1)} %bitcast.87), calls=%async_computation.4 | async-start | bytes 4194304
  54.1 3.5 %copy-start.3 = (bf16[1,1,128,1536]{3,2,1,0:T(8,128)(2,1)S(1)}, bf16[1,1,128,1536]{3,2,1,0:T(8,128)(2,1)}, u32[]{:S(2)}) copy-start(bf16[1,1,128,1536]{3,2,1,0:T(8,128)(2,1)} %param.12) | copy-start | bytes 1179652
  54.1 3.5 %slice-start.1 = ((s8[6291456]{0:T(1024)(128)(4,1)}), s8[4194304]{0:T(1024)(128)(4,1)S(1)}, s32[]{:S(2)}) async-start(s8[6291456]{0:T(1024)(128)(4,1)} %bitcast.87), calls=%async_computation.5 | async-start | bytes 8388608
  66.2 36.0 %all-to-all-start = ((bf16[8,16,4096]{2,1,0:T(8,128)(2,1)}), bf16[8,16,4096]{2,1,0:T(8,128)(2,1)S(1)}, u32[]{:S(2)}, u32[]{:S(2)}) async-start(bf16[8,16,4096]{2,1,0:T(8,128)(2,1)} %bitcast.92), calls=%async_computation | async-start | bytes 2097152 | tf_op jit(solution)/shard_map/all_to_all | solution.py:49
  102.2 1.0 copy-start
  104.5 7.8 %copy-start.2 = (f32[128,8]{1,0:T(8,128)S(1)}, f32[128,8]{1,0:T(8,128)}, u32[]{:S(2)}) copy-start(f32[128,8]{1,0:T(8,128)} %copy-done.1) | copy-start | bytes 12292
  120.1 9.8 %copy-start.4 = (bf16[1,1,128,1536]{3,2,1,0:T(8,128)(2,1)S(1)}, bf16[1,1,128,1536]{3,2,1,0:T(8,128)(2,1)}, u32[]{:S(2)}) copy-start(bf16[1,1,128,1536]{3,2,1,0:T(8,128)(2,1)} %param.12) | copy-start | bytes 1179652
Sparse Core Ops, SparseCore 0:
  54.2 110.1 reduce-scatter.1
where the time goes:
time: 172 us; the launch traced here: 171 us
  other arithmetic  38.7 us (23%)
  matrix products  35 us (20%)
  local copies, waits for them, and re-layouts  31.5 us (18%)
  waiting for transfers between devices  27.7 us (16%)
  blocking collectives  20.3 us (12%)
  between operations  14.2 us (8%)
  starting transfers between devices  3.82 us (2%)
    reduce_scatter x1, waiting for transfers between devices, shards(): lax.psum_scatter(lax.optimization_barrier(term.astype(jnp.bfloat16)).asty...  27.7 us
    all_to_all x1, blocking collectives, shards(): lax.all_to_all(outgoing.reshape(flight, CAP, D), 'expert', split_axis=0,...  20.3 us
    unnamed x20, local copies, waits for them, and re-layouts  15.1 us
    scatter x1, other arithmetic, shards(): jnp.zeros((flight * CAP + 1, D), jnp.bfloat16).at[slot_index].set(sent_rows)  11.8 us
    convert_element_type x1, other arithmetic, dequant(): return (quantized.astype(jnp.float32) * expanded).astype(jnp.bfloat16)  10.9 us
    unnamed x3, other arithmetic  9.21 us
    dot_general x1, matrix products, shards(): jnp.einsum('tkd,td->tk', picked, d_out, preferred_element_type=jnp.float32)  9.12 us
    dot_general x1, matrix products, shards(): jnp.dot(hidden, weight, preferred_element_type=jnp.float32)  8.57 us
  transfers between devices with their start and end apart: 2, of which 1 were waited for; matrix products, arithmetic and copies ran while one was open for 45% of the time, Pallas kernels for 0%

commit v1 on v0

v1 whole, which is shorter than its diff:
```python
import functools

import jax
import jax.numpy as jnp
from jax import lax
from jax.experimental import pallas as pl
from jax.experimental.pallas import tpu as pltpu
from jax.sharding import PartitionSpec as P

QB = 128
CAP = 16
VMEM_LIMIT = 48 * 1024 * 1024

bf16 = jnp.bfloat16
f32 = jnp.float32


def params():
    return pltpu.CompilerParams(vmem_limit_bytes=VMEM_LIMIT)


def vmem_spec():
    return pl.BlockSpec(memory_space=pltpu.VMEM)


def smem_spec():
    return pl.BlockSpec(memory_space=pltpu.SMEM)


def dispatch_kernel(flight, groups, cap_ref, hot_ref, ids_ref, probs_ref, dout_ref, full_ref, parts_ref, own_ref):
    tokens, topk = ids_ref.shape
    slots = flight * CAP
    lane = lax.broadcasted_iota(jnp.int32, (1, slots), 1)
    lane_expert = lane // CAP
    lane_rank = (lane % CAP).astype(f32)
    limit = jnp.zeros((1, slots), jnp.int32)
    for e in range(flight):
        hot = hot_ref[0, 0] == e
        for h in range(1, hot_ref.shape[1]):
            hot = jnp.logical_or(hot, hot_ref[0, h] == e)
        limit = jnp.where(lane_expert == e, jnp.where(hot, CAP, cap_ref[e]), limit)
    limit = limit.astype(f32)
    ids = ids_ref[...]
    probs = probs_ref[...]
    named = jnp.zeros((tokens, slots), f32)
    weight = jnp.zeros((tokens, slots), f32)
    for k in range(topk):
        hit = ids[:, k : k + 1] == lane_expert
        named = jnp.where(hit, 1.0, named)
        weight = jnp.where(hit, probs[:, k : k + 1], weight)
    row = lax.broadcasted_iota(jnp.int32, (tokens, tokens), 0)
    col = lax.broadcasted_iota(jnp.int32, (tokens, tokens), 1)
    before = (col < row).astype(f32).astype(bf16)
    rank = jnp.dot(before, named.astype(bf16), preferred_element_type=f32)
    owns = (named > 0.0) & (rank == lane_rank) & (rank < limit)
    own_weight = jnp.where(owns, weight, 0.0)
    own_ref[...] = own_weight
    owner = jnp.where(owns, 1.0, 0.0).T.astype(bf16)
    slot_weight = jnp.sum(own_weight.T, axis=1, keepdims=True)
    share = dout_ref.shape[1] // groups
    for g in range(groups):
        cols = pl.ds(g * share, share)
        rows = jnp.dot(owner, dout_ref[:, cols], preferred_element_type=f32)
        rows = (rows * slot_weight).astype(bf16)
        full_ref[:, cols] = rows
        parts_ref[g] = rows


def dispatch(capacity, hot_row, route_ids, route_probs, d_out, flight, groups):
    tokens, width = d_out.shape
    slots = flight * CAP
    return pl.pallas_call(
        functools.partial(dispatch_kernel, flight, groups),
        out_shape=(
            jax.ShapeDtypeStruct((slots, width), bf16),
            jax.ShapeDtypeStruct((groups, slots, width // groups), bf16),
            jax.ShapeDtypeStruct((tokens, slots), f32),
        ),
        in_specs=[smem_spec(), smem_spec(), vmem_spec(), vmem_spec(), vmem_spec()],
        out_specs=(vmem_spec(), vmem_spec(), vmem_spec()),
        compiler_params=params(),
        name="dispatch",
    )(capacity, hot_row, route_ids, route_probs, d_out)


def forward_kernel(block, scale_ref, gate_up_ref, quant_ref, hidden_ref, weight_ref, out_ref):
    step = pl.program_id(0)
    hid = hidden_ref.shape[1]

    @pl.when(step == 0)
    def _():
        gate = gate_up_ref[:, :hid].astype(f32)
        up = gate_up_ref[:, hid:].astype(f32)
        hidden_ref[...] = (gate * jax.nn.sigmoid(gate) * up).astype(bf16)

    for i in range(hid // QB):
        for j in range(block // QB):
            at = (pl.ds(i * QB, QB), pl.ds(j * QB, QB))
            scale = scale_ref[i, step * (block // QB) + j]
            weight_ref[at] = (quant_ref[at].astype(f32) * scale).astype(bf16)
    out_ref[...] = jnp.dot(hidden_ref[...], weight_ref[...], preferred_element_type=f32).astype(bf16)


def forward(w_scale, gate_up, w_quant, block=512):
    slots, double = gate_up.shape
    hid, width = w_quant.shape
    return pl.pallas_call(
        functools.partial(forward_kernel, block),
        grid=(width // block,),
        out_shape=(
            jax.ShapeDtypeStruct((slots, hid), bf16),
            jax.ShapeDtypeStruct((hid, width), bf16),
            jax.ShapeDtypeStruct((slots, width), bf16),
        ),
        in_specs=[
            smem_spec(),
            pl.BlockSpec((slots, double), lambda i: (0, 0)),
            pl.BlockSpec((hid, block), lambda i: (0, i)),
        ],
        out_specs=(
            pl.BlockSpec((slots, hid), lambda i: (0, 0)),
            pl.BlockSpec((hid, block), lambda i: (0, i)),
            pl.BlockSpec((slots, block), lambda i: (0, i)),
        ),
        compiler_params=params(),
        name="expert_forward",
    )(w_scale, gate_up, w_quant)


def backward_kernel(gate_up_ref, grads_ref, weight_ref, out_ref, acc_ref):
    step = pl.program_id(0)
    hid = acc_ref.shape[1]
    part = lax.dot_general(
        grads_ref[...], weight_ref[...], (((1,), (1,)), ((), ())), preferred_element_type=f32
    )

    @pl.when(step == 0)
    def _():
        acc_ref[...] = part

    @pl.when(step > 0)
    def _():
        acc_ref[...] += part

    @pl.when(step == pl.num_programs(0) - 1)
    def _():
        gate = gate_up_ref[:, :hid].astype(f32)
        up = gate_up_ref[:, hid:].astype(f32)
        sig = jax.nn.sigmoid(gate)
        d_hidden = acc_ref[...]
        out_ref[:, :hid] = (d_hidden * up * sig * (1.0 + gate * (1.0 - sig))).astype(bf16)
        out_ref[:, hid:] = (d_hidden * (gate * sig)).astype(bf16)


def backward(gate_up, grads, weight, block=1024):
    slots, double = gate_up.shape
    hid, width = weight.shape
    return pl.pallas_call(
        backward_kernel,
        grid=(width // block,),
        out_shape=jax.ShapeDtypeStruct((slots, double), bf16),
        in_specs=[
            pl.BlockSpec((slots, double), lambda i: (0, 0)),
            pl.BlockSpec((slots, block), lambda i: (0, i)),
            pl.BlockSpec((hid, block), lambda i: (0, i)),
        ],
        out_specs=pl.BlockSpec((slots, double), lambda i: (0, 0)),
        scratch_shapes=[pltpu.VMEM((slots, hid), f32)],
        compiler_params=params(),
        name="expert_backward",
    )(gate_up, grads, weight)


def combine_kernel(ids_ref, own_ref, dout_ref, ret_ref, out_ref, dprobs_ref, acc_ref):
    step = pl.program_id(0)
    tokens, topk = ids_ref.shape
    slots = own_ref.shape[1]
    own = own_ref[...]
    high = own.astype(bf16)
    low = (own - high.astype(f32)).astype(bf16)
    ret = ret_ref[...]
    out = jnp.dot(high, ret, preferred_element_type=f32)
    out = out + jnp.dot(low, ret, preferred_element_type=f32)
    out_ref[...] = out.astype(bf16)
    part = lax.dot_general(
        dout_ref[...], ret, (((1,), (1,)), ((), ())), preferred_element_type=f32
    )

    @pl.when(step == 0)
    def _():
        acc_ref[...] = part

    @pl.when(step > 0)
    def _():
        acc_ref[...] += part

    @pl.when(step == pl.num_programs(0) - 1)
    def _():
        inner = jnp.where(own > 0.0, acc_ref[...], 0.0)
        lane_expert = lax.broadcasted_iota(jnp.int32, (1, slots), 1) // CAP
        place = lax.broadcasted_iota(jnp.int32, (tokens, topk), 1)
        ids = ids_ref[...]
        result = jnp.zeros((tokens, topk), f32)
        for k in range(topk):
            mine = jnp.where(ids[:, k : k + 1] == lane_expert, inner, 0.0)
            result = jnp.where(place == k, jnp.sum(mine, axis=1, keepdims=True), result)
        dprobs_ref[...] = result


def combine(route_ids, own, d_out, returned, block=1024):
    tokens, width = d_out.shape
    topk = route_ids.shape[1]
    slots = own.shape[1]
    return pl.pallas_call(
        combine_kernel,
        grid=(width // block,),
        out_shape=(
            jax.ShapeDtypeStruct((tokens, width), bf16),
            jax.ShapeDtypeStruct((tokens, topk), f32),
        ),
        in_specs=[
            pl.BlockSpec((tokens, topk), lambda i: (0, 0)),
            pl.BlockSpec((tokens, slots), lambda i: (0, 0)),
            pl.BlockSpec((tokens, block), lambda i: (0, i)),
            pl.BlockSpec((slots, block), lambda i: (0, i)),
        ],
        out_specs=(
            pl.BlockSpec((tokens, block), lambda i: (0, i)),
            pl.BlockSpec((tokens, topk), lambda i: (0, 0)),
        ),
        scratch_shapes=[pltpu.VMEM((tokens, slots), f32)],
        compiler_params=params(),
        name="combine",
    )(route_ids, own, d_out, returned)


def weight_grad_kernel(grads_ref, hidden_ref, out_ref):
    out_ref[...] = lax.dot_general(
        grads_ref[...], hidden_ref[...], (((0,), (0,)), ((), ())), preferred_element_type=f32
    ).astype(bf16)


def weight_grad(grads, hidden, block=256):
    rows, share = grads.shape
    hid = hidden.shape[1]
    return pl.pallas_call(
        weight_grad_kernel,
        grid=(share // block,),
        out_shape=jax.ShapeDtypeStruct((share, hid), bf16),
        in_specs=[
            pl.BlockSpec((rows, block), lambda i: (0, i)),
            pl.BlockSpec((rows, hid), lambda i: (0, 0)),
        ],
        out_specs=pl.BlockSpec((block, hid), lambda i: (i, 0)),
        compiler_params=params(),
        name="weight_grad",
    )(grads, hidden)


def shards(route_ids, route_probs, capacity, hot_lists, gate_up, w_quant, w_scale, d_out):
    flight = lax.axis_size("expert")
    groups = lax.axis_size("dp")
    slots = flight * CAP
    width = d_out.shape[1]
    gate_up = gate_up[0, 0]
    full, parts, own = dispatch(
        capacity, hot_lists, route_ids, route_probs, d_out, flight, groups
    )
    crossed = lax.all_to_all(
        parts.reshape(groups * flight, CAP, width // groups),
        ("dp", "expert"),
        split_axis=0,
        concat_axis=0,
        tiled=True,
    )
    arrived = lax.all_to_all(
        full.reshape(flight, CAP, width), "expert", split_axis=0, concat_axis=0, tiled=True
    )
    hidden, weight, expert_out = forward(w_scale[0], gate_up, w_quant[0])
    hidden_all = lax.all_gather(hidden, "dp", axis=0, tiled=True)
    returned = lax.all_to_all(
        expert_out.reshape(flight, CAP, width), "expert", split_axis=0, concat_axis=0, tiled=True
    )
    d_gate_up = backward(gate_up, arrived.reshape(slots, width), weight)
    combined, d_probs = combine(route_ids, own, d_out, returned.reshape(slots, width))
    d_weight = weight_grad(crossed.reshape(groups * slots, width // groups), hidden_all)
    return (combined, d_probs, d_gate_up[None, None], d_weight[None])


def solution(mesh):
    placed = (
        P(("dp", "expert"), None),
        P(("dp", "expert"), None),
        P(),
        P("dp", None),
        P("dp", "expert", None, None),
        P("expert", None, None),
        P("expert", None, None),
        P(("dp", "expert"), None),
    )
    return jax.shard_map(
        shards,
        mesh=mesh,
        in_specs=placed,
        out_specs=(
            P(("dp", "expert"), None),
            P(("dp", "expert"), None),
            P("dp", "expert", None, None),
            P("expert", "dp", None),
        ),
        check_vma=False,
    )
```

time: 172 us -> 110 us (0.64)
  other arithmetic: 38.7 us -> 0 us
  blocking collectives: 20.3 us -> 58.4 us
  matrix products: 35 us -> 0 us
  waiting for transfers between devices: 27.7 us -> 3.46 us
  Pallas kernels: 0 us -> 23.4 us
  local copies, waits for them, and re-layouts: 31.5 us -> 14.2 us
  between operations: 14.2 us -> 0.67 us
  starting transfers between devices: 3.82 us -> 9.14 us
    all_gather x0 -> x1, blocking collectives: none -> 39.6 us  [shards(): hidden_all = lax.all_gather(hidden, 'dp', axis=0, tiled=True)]
    dot_general x5 -> x0, matrix products: 35 us -> none  [the longest x1 9.12 us: shards(): jnp.einsum('tkd,td->tk', picked, d_out, preferred_element_type=jnp.float32)]
    reduce_scatter x1 -> x0, waiting for transfers between devices: 27.7 us -> none  [shards(): lax.psum_scatter(lax.optimization_barrier(term.astype(jnp.bfloat16)).asty...]
    pallas_call x0 -> x5, Pallas kernels: none -> 23.4 us  [the longest x1 8.52 us: forward(): pl.pallas_call(functools.partial(forward_kernel, block), grid=(width // b...]
    convert_element_type x3 -> x0, other arithmetic: 12.3 us -> none  [the longest x1 10.9 us: dequant(): return (quantized.astype(jnp.float32) * expanded).astype(jnp.bfloat16)]
    scatter x1 -> x0, other arithmetic: 11.8 us -> none  [shards(): jnp.zeros((flight * CAP + 1, D), jnp.bfloat16).at[slot_index].set(sent_rows)]
    unnamed x3 -> x0, other arithmetic: 9.21 us -> none
    gather x1 -> x0, local copies, waits for them, and re-layouts: 7.74 us -> none  [shards(): picked = padded[slot_index].reshape(tokens_here, TOPK, D)]
  transfers between devices with their start and end apart: 2 -> 2, of which waited for: 1 -> 1; matrix products, arithmetic and copies ran while one was open for 45% -> 2% of each run, Pallas kernels for 0% -> 17%
where the time goes in v1:
time: 110 us; the launch traced here: 109 us
  blocking collectives  58.4 us (53%)
  Pallas kernels  23.4 us (21%)
  local copies, waits for them, and re-layouts  14.2 us (13%)
  starting transfers between devices  9.14 us (8%)
  waiting for transfers between devices  3.46 us (3%)
    all_gather x1, blocking collectives, shards(): hidden_all = lax.all_gather(hidden, 'dp', axis=0, tiled=True)  39.6 us
    all_to_all x1, blocking collectives, shards(): lax.all_to_all(expert_out.reshape(flight, CAP, width), 'expert', split_ax...  18.8 us
    unnamed x38, local copies, waits for them, and re-layouts  14.2 us
    pallas_call x1, Pallas kernels, forward(): pl.pallas_call(functools.partial(forward_kernel, block), grid=(width // b...  8.52 us
    pallas_call x1, Pallas kernels, backward(): pl.pallas_call(backward_kernel, grid=(width // block,), out_shape=jax.Sha...  6.03 us
    all_to_all x1, starting transfers between devices, shards(): lax.all_to_all(full.reshape(flight, CAP, width), 'expert', split_axis=0,...  5.17 us
    all_to_all x1, starting transfers between devices, shards(): lax.all_to_all(parts.reshape(groups * flight, CAP, width // groups), ('dp...  3.97 us
    pallas_call x1, Pallas kernels, combine(): pl.pallas_call(combine_kernel, grid=(width // block,), out_shape=(jax.Sha...  3.48 us
  transfers between devices with their start and end apart: 2, of which 1 were waited for; matrix products, arithmetic and copies ran while one was open for 2% of the time, Pallas kernels for 17%

profile of v1, /device:TPU:0, one launch (start us, length us, event | category | flops | bytes accessed | tf_op | source)
XLA Modules:
  0.0 109.2 jit_solution(1202866853214487617)
XLA Ops:
  0.6 0.8 copy.14.ids_ref
  1.4 0.8 copy.13.probs_ref
  2.2 1.2 %copy-done = bf16[128,4096]{1,0:T(8,128)(2,1)S(1)} copy-done((bf16[128,4096]{1,0:T(8,128)(2,1)S(1)}, bf16[128,4096]{1,0:T(8,128)(2,1)}, u32[]{:S(2)}) %copy-start) | copy-done | bytes 1048600
  3.5 0.7 copy-done.15
  4.1 0.7 copy-done.16
  4.8 2.5 %dispatch.1 = (bf16[128,4096]{1,0:T(8,128)(2,1)}, bf16[4,128,1024]{2,1,0:T(8,128)(2,1)S(1)}, f32[128,128]{1,0:T(8,128)S(1)}) custom-call(s32[8]{0:T(128)S(1)} %copy-done.15, s32[1,4]{1,0:T(1,128)S(1)} %copy-done.16, s32[128,8]{1,0:T(8,128)S(1)} %copy.14.ids_ref, f32[128,8]{1,0:T(8,128)S(1)} %copy.13.probs_ref, bf16[128,4096]{1,0:T(8,128)(2,1)S(1)} %copy-done), custom_call_target="tpu_custom_call" | custom-call | tf_op jit(solution)/shard_map/dispatch/pallas_call | solution.py:72
  7.2 1.0 copy-done.7
  8.8 5.2 %all-to-all-start.1 = ((bf16[8,16,4096]{2,1,0:T(8,128)(2,1)}), bf16[8,16,4096]{2,1,0:T(8,128)(2,1)S(1)}, u32[]{:S(2)}, u32[]{:S(2)}) async-start(bf16[8,16,4096]{2,1,0:T(8,128)(2,1)} %bitcast.4), calls=%async_computation.1 | async-start | bytes 2097152 | tf_op jit(solution)/shard_map/all_to_all | solution.py:276
  14.0 0.8 copy.18
  14.8 1.0 copy-done.5
  15.8 8.5 %expert_forward.1 = (bf16[128,768]{1,0:T(8,128)(2,1)S(1)}, bf16[768,4096]{1,0:T(8,128)(2,1)}, bf16[128,4096]{1,0:T(8,128)(2,1)S(1)}) custom-call(f32[6,32]{1,0:T(8,128)S(1)} %bitcast.20, bf16[128,1536]{1,0:T(8,128)(2,1)S(1)} %bitcast.16, bf16[768,4096]{1,0:T(8,128)(2,1)} %bitcast.21), custom_call_target="tpu_custom_call" | custom-call | tf_op jit(solution)/shard_map/expert_forward/pallas_call | solution.py:107
  24.3 1.0 copy-done.8
  25.3 0.7 copy-done.11
  25.9 3.5 %all-to-all-done.1 = bf16[8,16,4096]{2,1,0:T(8,128)(2,1)S(1)} async-done(((bf16[8,16,4096]{2,1,0:T(8,128)(2,1)}), bf16[8,16,4096]{2,1,0:T(8,128)(2,1)S(1)}, u32[]{:S(2)}, u32[]{:S(2)}) %all-to-all-start.1) | async-done | bytes 1048608 | tf_op jit(solution)/shard_map/all_to_all | solution.py:276
  29.4 18.8 %all_to_all.15 = bf16[8,16,4096]{2,1,0:T(8,128)(2,1)S(1)} all-to-all(bf16[8,16,4096]{2,1,0:T(8,128)(2,1)} %bitcast.19), channel_id=1, replica_groups=mesh['dp'=4,'expert'=8] {'expert'}, dimensions={0} | all-to-all | bytes 2097152 | tf_op jit(solution)/shard_map/all_to_all | solution.py:281
  48.2 4.0 %all-to-all-start.2 = ((bf16[32,16,1024]{2,1,0:T(8,128)(2,1)}), bf16[32,16,1024]{2,1,0:T(8,128)(2,1)S(1)}, u32[]{:S(2)}, u32[]{:S(2)}) async-start(bf16[32,16,1024]{2,1,0:T(8,128)(2,1)} %bitcast.18), calls=%async_computation.2 | async-start | bytes 2097152 | tf_op jit(solution)/shard_map/all_to_all | solution.py:269
  52.2 39.6 %all_gather.3.hidden_ref = bf16[512,768]{1,0:T(8,128)(2,1)} all-gather(bf16[128,768]{1,0:T(8,128)(2,1)} %copy-done.11), channel_id=1, replica_groups=mesh['dp'=4,'expert'=8] {'dp'}, dimensions={0}, use_global_device_ids=true | all-gather | bytes 983040 | tf_op jit(solution)/shard_map/all_gather | solution.py:280
  91.8 0.8 copy-done.10
  92.6 0.8 copy-done.13
  93.5 3.5 %combine.1 = (bf16[128,4096]{1,0:T(8,128)(2,1)}, f32[128,8]{1,0:T(8,128)S(1)}) custom-call(s32[128,8]{1,0:T(8,128)S(1)} %copy-done.10, f32[128,128]{1,0:T(8,128)S(1)} %copy-done.13, bf16[128,4096]{1,0:T(8,128)(2,1)S(1)} %copy-done.1, bf16[128,4096]{1,0:T(8,128)(2,1)S(1)} %bitcast.14), custom_call_target="tpu_custom_call" | custom-call | tf_op jit(solution)/shard_map/combine/pallas_call | solution.py:214
  97.6 1.5 %copy.15 = f32[128,8]{0,1:T(8,128)} copy(f32[128,8]{1,0:T(8,128)} %copy-done.14) | data formatting | bytes 8192
  99.1 1.2 %copy-done.3 = bf16[8,16,4096]{2,1,0:T(8,128)(2,1)S(1)} copy-done((bf16[8,16,4096]{2,1,0:T(8,128)(2,1)S(1)}, bf16[8,16,4096]{2,1,0:T(8,128)(2,1)}, u32[]{:S(2)}) %copy-start.3) | copy-done | bytes 1048600
  100.3 6.0 %expert_backward.1 = bf16[128,1536]{1,0:T(8,128)(2,1)} custom-call(bf16[128,1536]{1,0:T(8,128)(2,1)S(1)} %bitcast.17, bf16[128,4096]{1,0:T(8,128)(2,1)S(1)} %bitcast.15, bf16[768,4096]{1,0:T(8,128)(2,1)} %get-tuple-element.17.weight_ref), custom_call_target="tpu_custom_call" | custom-call | tf_op jit(solution)/shard_map/expert_backward/pallas_call | solution.py:158
  106.3 2.9 %weight_grad.1 = bf16[1024,768]{1,0:T(8,128)(2,1)} custom-call(bf16[512,1024]{1,0:T(8,128)(2,1)S(1)} %bitcast.13, bf16[512,768]{1,0:T(8,128)(2,1)S(1)} %copy-done.4), custom_call_target="tpu_custom_call" | custom-call | tf_op jit(solution)/shard_map/weight_grad/pallas_call | solution.py:246
  (25 shorter events, 1.3 us)
Async XLA Ops:
  1.4 6.8 %copy-start.9 = (s32[128,8]{1,0:T(8,128)}, s32[128,8]{1,0:T(8,128)S(1)}, u32[]{:S(2)}) copy-start(s32[128,8]{1,0:T(8,128)S(1)} %copy.14.ids_ref) | copy-start | bytes 12292
  2.2 1.2 %copy-start = (bf16[128,4096]{1,0:T(8,128)(2,1)S(1)}, bf16[128,4096]{1,0:T(8,128)(2,1)}, u32[]{:S(2)}) copy-start(bf16[128,4096]{1,0:T(8,128)(2,1)} %dout_ref.3) | copy-start | bytes 3145732
  3.5 0.7 copy-start.15
  4.1 0.7 copy-start.16
  7.2 1.0 copy-start.7
  8.2 0.6 copy-start.12
  8.8 20.6 %all-to-all-start.1 = ((bf16[8,16,4096]{2,1,0:T(8,128)(2,1)}), bf16[8,16,4096]{2,1,0:T(8,128)(2,1)S(1)}, u32[]{:S(2)}, u32[]{:S(2)}) async-start(bf16[8,16,4096]{2,1,0:T(8,128)(2,1)} %bitcast.4), calls=%async_computation.1 | async-start | bytes 2097152 | tf_op jit(solution)/shard_map/all_to_all | solution.py:276
  14.0 77.8 %copy-start.1 = (bf16[128,4096]{1,0:T(8,128)(2,1)S(1)}, bf16[128,4096]{1,0:T(8,128)(2,1)}, u32[]{:S(2)}) copy-start(bf16[128,4096]{1,0:T(8,128)(2,1)} %dout_ref.3) | copy-start | bytes 3145732
  14.8 1.0 copy-start.5
  15.8 83.3 %copy-start.6 = (bf16[1,1,128,1536]{3,2,1,0:T(8,128)(2,1)S(1)}, bf16[1,1,128,1536]{3,2,1,0:T(8,128)(2,1)}, u32[]{:S(2)}) copy-start(bf16[1,1,128,1536]{3,2,1,0:T(8,128)(2,1)} %param.12) | copy-start | bytes 1179652
  24.3 1.0 copy-start.8
  25.3 0.7 copy-start.11
  29.4 18.8 %copy-start.2 = (bf16[8,16,4096]{2,1,0:T(8,128)(2,1)}, bf16[8,16,4096]{2,1,0:T(8,128)(2,1)S(1)}, u32[]{:S(2)}) copy-start(bf16[8,16,4096]{2,1,0:T(8,128)(2,1)S(1)} %all-to-all-done.1) | copy-start | bytes 3145732
  48.2 58.1 %all-to-all-start.2 = ((bf16[32,16,1024]{2,1,0:T(8,128)(2,1)}), bf16[32,16,1024]{2,1,0:T(8,128)(2,1)S(1)}, u32[]{:S(2)}, u32[]{:S(2)}) async-start(bf16[32,16,1024]{2,1,0:T(8,128)(2,1)} %bitcast.18), calls=%async_computation.2 | async-start | bytes 2097152 | tf_op jit(solution)/shard_map/all_to_all | solution.py:269
  91.8 0.8 copy-start.10
  92.6 0.8 copy-start.13
  96.9 0.6 copy-start.14
  99.1 1.2 %copy-start.3 = (bf16[8,16,4096]{2,1,0:T(8,128)(2,1)S(1)}, bf16[8,16,4096]{2,1,0:T(8,128)(2,1)}, u32[]{:S(2)}) copy-start(bf16[8,16,4096]{2,1,0:T(8,128)(2,1)} %copy-done.2) | copy-start | bytes 3145732
  100.3 6.0 %copy-start.4 = (bf16[512,768]{1,0:T(8,128)(2,1)S(1)}, bf16[512,768]{1,0:T(8,128)(2,1)}, u32[]{:S(2)}) copy-start(bf16[512,768]{1,0:T(8,128)(2,1)} %all_gather.3.hidden_ref) | copy-start | bytes 2359300

commit v2 on v0

v2 whole, which is shorter than its diff:
```python
import functools

import jax
import jax.numpy as jnp
from jax import lax
from jax.experimental import pallas as pl
from jax.experimental.pallas import tpu as pltpu
from jax.sharding import PartitionSpec as P

QB = 128
CAP = 16
VMEM_LIMIT = 40 * 1024 * 1024

bf16 = jnp.bfloat16
f32 = jnp.float32

VMEM = pl.BlockSpec(memory_space=pltpu.VMEM)
SMEM = pl.BlockSpec(memory_space=pltpu.SMEM)
ANY = pl.BlockSpec(memory_space=pl.ANY)


def params():
    return pltpu.CompilerParams(vmem_limit_bytes=VMEM_LIMIT)


def cost(flops, moved):
    return pl.CostEstimate(flops=flops, bytes_accessed=moved, transcendentals=0)


def chunks(total, size):
    return [pl.ds(start, size) for start in range(0, total, size)]


def hidden_kernel(gate_up_ref, out_ref):
    hid = out_ref.shape[1]
    gate = gate_up_ref[:, :hid].astype(f32)
    up = gate_up_ref[:, hid:].astype(f32)
    out_ref[...] = (gate * jax.nn.sigmoid(gate) * up).astype(bf16)


def make_hidden(gate_up):
    slots, double = gate_up.shape
    return pl.pallas_call(
        hidden_kernel,
        out_shape=pltpu.HBM((slots, double // 2), bf16),
        in_specs=[VMEM],
        out_specs=VMEM,
        compiler_params=params(),
        name="hidden",
    )(gate_up)


def dispatch_kernel(flight, groups, cap_ref, hot_ref, ids_ref, probs_ref, dout_ref, own_ref, parts_ref, *full_refs):
    topk, tokens = ids_ref.shape
    slots = flight * CAP
    me = lax.axis_index("expert")
    row = lax.broadcasted_iota(jnp.int32, (slots, 1), 0)
    row_expert = (row // CAP) ^ me
    row_rank = (row % CAP).astype(f32)
    limit = jnp.zeros((slots, 1), jnp.int32)
    for e in range(flight):
        hot = hot_ref[0, 0] == e
        for h in range(1, hot_ref.shape[1]):
            hot = jnp.logical_or(hot, hot_ref[0, h] == e)
        limit = jnp.where(row_expert == e, jnp.where(hot, CAP, cap_ref[e]), limit)
    limit = limit.astype(f32)
    named = jnp.zeros((slots, tokens), f32)
    weight = jnp.zeros((slots, tokens), f32)
    for k in range(topk):
        hit = ids_ref[k : k + 1, :] == row_expert
        named = jnp.where(hit, 1.0, named)
        weight = jnp.where(hit, probs_ref[k : k + 1, :], weight)
    first = lax.broadcasted_iota(jnp.int32, (tokens, tokens), 0)
    second = lax.broadcasted_iota(jnp.int32, (tokens, tokens), 1)
    before = (first < second).astype(f32).astype(bf16)
    rank = jnp.dot(named.astype(bf16), before, preferred_element_type=f32)
    owns = (named > 0.0) & (rank == row_rank) & (rank < limit)
    own_weight = jnp.where(owns, weight, 0.0)
    own_ref[...] = own_weight
    owner = jnp.where(owns, 1.0, 0.0).astype(bf16)
    slot_weight = jnp.sum(own_weight, axis=1, keepdims=True)
    share = dout_ref.shape[1] // groups
    for g in range(groups):
        cols = pl.ds(g * share, share)
        rows = jnp.dot(owner, dout_ref[:, cols], preferred_element_type=f32)
        rows = (rows * slot_weight).astype(bf16)
        for j in range(flight):
            block = rows[j * CAP : (j + 1) * CAP, :]
            full_refs[j][:, cols] = block
            parts_ref[g, pl.ds(pl.multiple_of((me ^ j) * CAP, CAP), CAP), :] = block


def dispatch(capacity, hot_row, ids, probs, d_out, flight, groups):
    tokens, width = d_out.shape
    slots = flight * CAP
    return pl.pallas_call(
        functools.partial(dispatch_kernel, flight, groups),
        out_shape=(
            jax.ShapeDtypeStruct((slots, tokens), f32),
            pltpu.HBM((groups, slots, width // groups), bf16),
        )
        + (pltpu.HBM((CAP, width), bf16),) * flight,
        in_specs=[SMEM, SMEM, VMEM, VMEM, VMEM],
        out_specs=(VMEM,) * (2 + flight),
        compiler_params=params(),
        name="dispatch",
    )(capacity, hot_row, ids, probs, d_out)


def forward_kernel(flight, block, scale_ref, hidden_ref, quant_ref, tie_ref, weight_ref, *refs):
    out_refs, (quant, rows, sems) = refs[:flight], refs[flight:]
    hid, width = quant.shape
    me = lax.axis_index("expert")
    copies = [
        pltpu.make_async_copy(quant_ref.at[:, cols], quant.at[:, cols], sems.at[c])
        for c, cols in enumerate(chunks(width, block))
    ]
    for copy in copies:
        copy.start()
    for j in range(flight):
        rows[pl.ds(j * CAP, CAP), :] = hidden_ref[pl.ds(pl.multiple_of((me ^ j) * CAP, CAP), CAP), :]
    for c, cols in enumerate(chunks(width, block)):
        copies[c].wait()
        for i in range(hid // QB):
            for j in range(block // QB):
                at = (pl.ds(i * QB, QB), pl.ds(c * block + j * QB, QB))
                scale = scale_ref[i, 0, c * (block // QB) + j]
                weight_ref[at] = (quant[at].astype(f32) * scale).astype(bf16)
        out = jnp.dot(rows[...], weight_ref[:, cols], preferred_element_type=f32).astype(bf16)
        for j in range(flight):
            out_refs[j][:, cols] = out[j * CAP : (j + 1) * CAP, :]


def forward(scale, hidden, quant, tie, flight, block=512):
    hid, width = quant.shape
    return pl.pallas_call(
        functools.partial(forward_kernel, flight, block),
        out_shape=(jax.ShapeDtypeStruct((hid, width), bf16),)
        + (pltpu.HBM((CAP, width), bf16),) * flight,
        in_specs=[SMEM, VMEM, ANY, ANY],
        out_specs=(VMEM,) * (1 + flight),
        scratch_shapes=[
            pltpu.VMEM((hid, width), bf16),
            pltpu.VMEM((flight * CAP, hid), bf16),
            pltpu.SemaphoreType.DMA((width // block,)),
        ],
        compiler_params=params(),
        name="expert_forward",
    )(scale, hidden, quant, tie)


def backward_kernel(flight, block, gate_up_ref, weight_ref, *refs):
    in_refs, (out_ref, grads, acc) = refs[:flight], refs[flight:]
    hid, width = weight_ref.shape
    me = lax.axis_index("expert")
    for j in range(flight):
        grads[pl.ds(pl.multiple_of((me ^ j) * CAP, CAP), CAP), :] = in_refs[j][...]
    for c, cols in enumerate(chunks(width, block)):
        part = lax.dot_general(
            grads[:, cols], weight_ref[:, cols], (((1,), (1,)), ((), ())), preferred_element_type=f32
        )
        if c == 0:
            acc[...] = part
        else:
            acc[...] += part
    gate = gate_up_ref[:, :hid].astype(f32)
    up = gate_up_ref[:, hid:].astype(f32)
    sig = jax.nn.sigmoid(gate)
    d_hidden = acc[...]
    out_ref[:, :hid] = (d_hidden * up * sig * (1.0 + gate * (1.0 - sig))).astype(bf16)
    out_ref[:, hid:] = (d_hidden * (gate * sig)).astype(bf16)


def backward(gate_up, weight, arrived, block=1024):
    slots, double = gate_up.shape
    hid, width = weight.shape
    flight = len(arrived)
    return pl.pallas_call(
        functools.partial(backward_kernel, flight, block),
        out_shape=jax.ShapeDtypeStruct((slots, double), bf16),
        in_specs=[VMEM] * (2 + flight),
        out_specs=VMEM,
        scratch_shapes=[pltpu.VMEM((slots, width), bf16), pltpu.VMEM((slots, hid), f32)],
        compiler_params=params(),
        name="expert_backward",
    )(gate_up, weight, *arrived)


def combine_kernel(flight, block, ids_ref, own_ref, dout_ref, *refs):
    ret_refs, (out_ref, dprobs_ref, ret) = refs[:flight], refs[flight:]
    topk, tokens = ids_ref.shape
    width = dout_ref.shape[1]
    slots = flight * CAP
    me = lax.axis_index("expert")
    for j in range(flight):
        ret[pl.ds(j * CAP, CAP), :] = ret_refs[j][...]
    own = own_ref[...]
    turned = own.T
    high = turned.astype(bf16)
    low = (turned - high.astype(f32)).astype(bf16)
    total = jnp.zeros((slots, tokens), f32)
    for cols in chunks(width, block):
        here = ret[:, cols]
        out = jnp.dot(high, here, preferred_element_type=f32)
        out = out + jnp.dot(low, here, preferred_element_type=f32)
        out_ref[:, cols] = out.astype(bf16)
        total = total + lax.dot_general(
            here, dout_ref[:, cols], (((1,), (1,)), ((), ())), preferred_element_type=f32
        )
    inner = jnp.where(own > 0.0, total, 0.0)
    row_expert = (lax.broadcasted_iota(jnp.int32, (slots, 1), 0) // CAP) ^ me
    for k in range(topk):
        mine = jnp.where(ids_ref[k : k + 1, :] == row_expert, inner, 0.0)
        dprobs_ref[k : k + 1, :] = jnp.sum(mine, axis=0, keepdims=True)


def combine(ids, own, d_out, returned, block=1024):
    tokens, width = d_out.shape
    slots = own.shape[0]
    flight = len(returned)
    return pl.pallas_call(
        functools.partial(combine_kernel, flight, block),
        out_shape=(
            jax.ShapeDtypeStruct((tokens, width), bf16),
            jax.ShapeDtypeStruct(ids.shape, f32),
        ),
        in_specs=[VMEM] * (3 + flight),
        out_specs=(VMEM, VMEM),
        scratch_shapes=[pltpu.VMEM((slots, width), bf16)],
        compiler_params=params(),
        name="combine",
    )(ids, own, d_out, *returned)


def weight_grad_kernel(groups, block, grads_ref, *refs):
    hid_refs, (out_ref, hidden) = refs[:groups], refs[groups:]
    rows, share = grads_ref.shape
    slots = rows // groups
    me = lax.axis_index("dp")
    for j in range(groups):
        hidden[pl.ds(pl.multiple_of((me ^ j) * slots, slots), slots), :] = hid_refs[j][...]
    for cols in chunks(share, block):
        out_ref[cols, :] = lax.dot_general(
            grads_ref[:, cols], hidden[...], (((0,), (0,)), ((), ())), preferred_element_type=f32
        ).astype(bf16)


def weight_grad(grads, hiddens, block=256):
    rows, share = grads.shape
    hid = hiddens[0].shape[1]
    groups = len(hiddens)
    return pl.pallas_call(
        functools.partial(weight_grad_kernel, groups, block),
        out_shape=jax.ShapeDtypeStruct((share, hid), bf16),
        in_specs=[VMEM] * (1 + groups),
        out_specs=VMEM,
        scratch_shapes=[pltpu.VMEM((rows, hid), bf16)],
        compiler_params=params(),
        name="weight_grad",
    )(grads, *hiddens)


def swap(value, axis, j):
    size = lax.axis_size(axis)
    return lax.ppermute(value, axis, [(i, i ^ j) for i in range(size)])


def shards(route_ids, route_probs, capacity, hot_lists, gate_up, w_quant, w_scale, d_out):
    flight = lax.axis_size("expert")
    groups = lax.axis_size("dp")
    slots = flight * CAP
    width = d_out.shape[1]
    gate_up = gate_up[0, 0]
    ids, probs = route_ids.T, route_probs.T
    hidden = make_hidden(gate_up)
    hiddens = [hidden] + [swap(hidden, "dp", j) for j in range(1, groups)]
    own, parts, *full = dispatch(capacity, hot_lists, ids, probs, d_out, flight, groups)
    crossed = lax.all_to_all(
        parts.reshape(groups * flight, CAP, width // groups),
        ("dp", "expert"),
        split_axis=0,
        concat_axis=0,
        tiled=True,
    )
    arrived = [full[0]] + [swap(full[j], "expert", j) for j in range(1, flight)]
    weight, *expert_out = forward(
        w_scale.transpose(1, 0, 2), hidden, w_quant[0], own, flight
    )
    returned = [expert_out[0]] + [swap(expert_out[j], "expert", j) for j in range(1, flight)]
    d_gate_up = backward(gate_up, weight, arrived)
    combined, d_probs = combine(ids, own, d_out, returned)
    d_weight = weight_grad(crossed.reshape(groups * slots, width // groups), hiddens)
    return (combined, d_probs.T, d_gate_up[None, None], d_weight[None])


def solution(mesh):
    placed = (
        P(("dp", "expert"), None),
        P(("dp", "expert"), None),
        P(),
        P("dp", None),
        P("dp", "expert", None, None),
        P("expert", None, None),
        P("expert", None, None),
        P(("dp", "expert"), None),
    )
    return jax.shard_map(
        shards,
        mesh=mesh,
        in_specs=placed,
        out_specs=(
            P(("dp", "expert"), None),
            P(("dp", "expert"), None),
            P("dp", "expert", None, None),
            P("expert", "dp", None),
        ),
        check_vma=False,
    )
```

time: 172 us -> 73.4 us (0.43)
  other arithmetic: 38.7 us -> 0 us
  matrix products: 35 us -> 0 us
  local copies, waits for them, and re-layouts: 31.5 us -> 9.28 us
  starting transfers between devices: 3.82 us -> 25.2 us
  blocking collectives: 20.3 us -> 0 us
  Pallas kernels: 0 us -> 18.4 us
  between operations: 14.2 us -> 0.72 us
  waiting for transfers between devices: 27.7 us -> 19.3 us
    dot_general x5 -> x0, matrix products: 35 us -> none  [the longest x1 9.12 us: shards(): jnp.einsum('tkd,td->tk', picked, d_out, preferred_element_type=jnp.float32)]
    reduce_scatter x1 -> x0, waiting for transfers between devices: 27.7 us -> none  [shards(): lax.psum_scatter(lax.optimization_barrier(term.astype(jnp.bfloat16)).asty...]
    all_to_all x1 -> x0, blocking collectives: 20.3 us -> none  [shards(): lax.all_to_all(outgoing.reshape(flight, CAP, D), 'expert', split_axis=0,...]
    ppermute x0 -> x17, waiting for transfers between devices: none -> 19.3 us  [swap(): return lax.ppermute(value, axis, [(i, i ^ j) for i in range(size)])]
    pallas_call x0 -> x6, Pallas kernels: none -> 18.4 us  [the longest x1 7.09 us: forward(): pl.pallas_call(functools.partial(forward_kernel, flight, block), out_shap...]
    ppermute x0 -> x17, starting transfers between devices: none -> 17.9 us  [swap(): return lax.ppermute(value, axis, [(i, i ^ j) for i in range(size)])]
    convert_element_type x3 -> x0, other arithmetic: 12.3 us -> none  [the longest x1 10.9 us: dequant(): return (quantized.astype(jnp.float32) * expanded).astype(jnp.bfloat16)]
    scatter x1 -> x0, other arithmetic: 11.8 us -> none  [shards(): jnp.zeros((flight * CAP + 1, D), jnp.bfloat16).at[slot_index].set(sent_rows)]
  transfers between devices with their start and end apart: 2 -> 18, of which waited for: 1 -> 9; matrix products, arithmetic and copies ran while one was open for 45% -> 0% of each run, Pallas kernels for 0% -> 18%
where the time goes in v2:
time: 73.4 us; the launch traced here: 72.9 us
  starting transfers between devices  25.2 us (34%)
  waiting for transfers between devices  19.3 us (26%)
  Pallas kernels  18.4 us (25%)
  local copies, waits for them, and re-layouts  9.28 us (13%)
    ppermute x17, waiting for transfers between devices, swap(): return lax.ppermute(value, axis, [(i, i ^ j) for i in range(size)])  19.3 us
    ppermute x17, starting transfers between devices, swap(): return lax.ppermute(value, axis, [(i, i ^ j) for i in range(size)])  17.9 us
    unnamed x30, local copies, waits for them, and re-layouts  9.28 us
    all_to_all x1, starting transfers between devices, shards(): lax.all_to_all(parts.reshape(groups * flight, CAP, width // groups), ('dp...  7.3 us
    pallas_call x1, Pallas kernels, forward(): pl.pallas_call(functools.partial(forward_kernel, flight, block), out_shap...  7.09 us
    pallas_call x1, Pallas kernels, weight_grad(): pl.pallas_call(functools.partial(weight_grad_kernel, groups, block), out_...  3.12 us
    pallas_call x1, Pallas kernels, backward(): pl.pallas_call(functools.partial(backward_kernel, flight, block), out_sha...  2.99 us
    pallas_call x1, Pallas kernels, dispatch(): pl.pallas_call(functools.partial(dispatch_kernel, flight, groups), out_sh...  2.4 us
  transfers between devices with their start and end apart: 18, of which 9 were waited for; matrix products, arithmetic and copies ran while one was open for 0% of the time, Pallas kernels for 18%

profile of v2, /device:TPU:0, one launch (start us, length us, event | category | flops | bytes accessed | tf_op | source)
XLA Modules:
  0.0 72.9 jit_solution(17264859504606139663)
XLA Ops:
  0.6 1.2 %copy-done.1 = bf16[128,4096]{1,0:T(8,128)(2,1)S(1)} copy-done((bf16[128,4096]{1,0:T(8,128)(2,1)S(1)}, bf16[128,4096]{1,0:T(8,128)(2,1)}, u32[]{:S(2)}) %copy-start.1) | copy-done | bytes 1048600
  4.6 2.4 %dispatch.1 = (f32[128,128]{1,0:T(8,128)S(1)}, bf16[4,128,1024]{2,1,0:T(8,128)(2,1)}, bf16[16,4096]{1,0:T(8,128)(2,1)}, bf16[16,4096]{1,0:T(8,128)(2,1)}, bf16[1...) custom-call(s32[8]{0:T(128)S(1)} %copy-done.11, ...), custom_call_target="tpu_custom_call" | custom-call | tf_op jit(solution)/shard_map/dispatch/pallas_call | solution.py:96
  7.0 7.3 %all-to-all-start = ((bf16[32,16,1024]{2,1,0:T(8,128)(2,1)}), bf16[32,16,1024]{2,1,0:T(8,128)(2,1)S(1)}, u32[]{:S(2)}, u32[]{:S(2)}) async-start(bf16[32,16,1024]{2,1,0:T(8,128)(2,1)} %bitcast.19), calls=%async_computation | async-start | bytes 2097152 | tf_op jit(solution)/shard_map/all_to_all | solution.py:278
  14.3 1.8 %collective-permute-start.10 = (bf16[16,4096]{1,0:T(8,128)(2,1)}, bf16[16,4096]{1,0:T(8,128)(2,1)S(1)}, u32[]{:S(2)}, u32[]{:S(2)}) collective-permute-start(bf16[16,4096]{1,0:T(8,128)(2,1)} %get-tuple-element.41), channel_id=1, source_target_pairs={{0,4},{1,5},{2,6},{3,7},{4,0},{5,1},{6,2},{7,3},{8,12},{9,13},{10,... | collective-permute-start | bytes 393224 | tf_op jit(solution)/shard_map/ppermute | solution.py:265
  16.1 2.4 %collective-permute-start.12 = (bf16[16,4096]{1,0:T(8,128)(2,1)}, bf16[16,4096]{1,0:T(8,128)(2,1)S(1)}, u32[]{:S(2)}, u32[]{:S(2)}) collective-permute-start(bf16[16,4096]{1,0:T(8,128)(2,1)} %get-tuple-element.43), channel_id=1, source_target_pairs={{0,6},{1,7},{2,4},{3,5},{4,2},{5,3},{6,0},{7,1},{8,14},{9,15},{10,... | collective-permute-start | bytes 393224 | tf_op jit(solution)/shard_map/ppermute | solution.py:265
  19.2 1.0 %copy-done.3 = bf16[1,1,128,1536]{3,2,1,0:T(8,128)(2,1)S(1)} copy-done((bf16[1,1,128,1536]{3,2,1,0:T(8,128)(2,1)S(1)}, bf16[1,1,128,1536]{3,2,1,0:T(8,128)(2,1)}, u32[]{:S(2)}) %copy-start.3) | copy-done | bytes 393240
  20.9 2.8 %copy-done = bf16[1,768,4096]{2,1,0:T(8,128)(2,1)S(1)} copy-done((bf16[1,768,4096]{2,1,0:T(8,128)(2,1)S(1)}, bf16[1,768,4096]{2,1,0:T(8,128)(2,1)}, u32[]{:S(2)}) %copy-start) | copy-done | bytes 6291480
  24.4 7.1 %expert_forward.1 = (bf16[768,4096]{1,0:T(8,128)(2,1)S(1)}, bf16[16,4096]{1,0:T(8,128)(2,1)}, bf16[16,4096]{1,0:T(8,128)(2,1)}, bf16[16,4096]{1,0:T(8,128)(2,1)}...) custom-call(f32[6,1,32]{2,1,0:T(1,128)S(1)} %bitcast.17, ...), custom_call_target="tpu_custom_call" | custom-call | tf_op jit(solution)/shard_map/expert_forward/pallas_call | solution.py:136
  31.5 4.4 %collective-permute-done.10.refs_4_ = bf16[16,4096]{1,0:T(8,128)(2,1)S(1)} collective-permute-done((bf16[16,4096]{1,0:T(8,128)(2,1)}, bf16[16,4096]{1,0:T(8,128)(2,1)S(1)}, u32[]{:S(2)}, u32[]{:S(2)}) %collective-permute-start.10) | collective-permute-done | bytes 131104 | tf_op jit(solution)/shard_map/ppermute | solution.py:265
  35.9 2.6 %collective-permute-done.11.refs_5_ = bf16[16,4096]{1,0:T(8,128)(2,1)S(1)} collective-permute-done((bf16[16,4096]{1,0:T(8,128)(2,1)}, bf16[16,4096]{1,0:T(8,128)(2,1)S(1)}, u32[]{:S(2)}, u32[]{:S(2)}) %collective-permute-start.11) | collective-permute-done | bytes 131104 | tf_op jit(solution)/shard_map/ppermute | solution.py:265
  38.4 2.1 %collective-permute-start.1 = (bf16[16,4096]{1,0:T(8,128)(2,1)}, bf16[16,4096]{1,0:T(8,128)(2,1)S(1)}, u32[]{:S(2)}, u32[]{:S(2)}) collective-permute-start(bf16[16,4096]{1,0:T(8,128)(2,1)} %get-tuple-element.28), channel_id=1, source_target_pairs={{0,2},{1,3},{2,0},{3,1},{4,6},{5,7},{6,4},{7,5},{8,10},{9,11},{10,... | collective-permute-start | bytes 393224 | tf_op jit(solution)/shard_map/ppermute | solution.py:265
  40.8 1.3 %collective-permute-start.4 = (bf16[16,4096]{1,0:T(8,128)(2,1)}, bf16[16,4096]{1,0:T(8,128)(2,1)S(1)}, u32[]{:S(2)}, u32[]{:S(2)}) collective-permute-start(bf16[16,4096]{1,0:T(8,128)(2,1)} %get-tuple-element.31), channel_id=1, source_target_pairs={{0,5},{1,4},{2,7},{3,6},{4,1},{5,0},{6,3},{7,2},{8,13},{9,12},{10,... | collective-permute-start | bytes 393224 | tf_op jit(solution)/shard_map/ppermute | solution.py:265
  42.0 1.8 %collective-permute-start.5 = (bf16[16,4096]{1,0:T(8,128)(2,1)}, bf16[16,4096]{1,0:T(8,128)(2,1)S(1)}, u32[]{:S(2)}, u32[]{:S(2)}) collective-permute-start(bf16[16,4096]{1,0:T(8,128)(2,1)} %get-tuple-element.32), channel_id=1, source_target_pairs={{0,6},{1,7},{2,4},{3,5},{4,2},{5,3},{6,0},{7,1},{8,14},{9,15},{10,... | collective-permute-start | bytes 393224 | tf_op jit(solution)/shard_map/ppermute | solution.py:265
  43.8 1.3 %collective-permute-done.1.refs_2_ = bf16[16,4096]{1,0:T(8,128)(2,1)S(1)} collective-permute-done((bf16[16,4096]{1,0:T(8,128)(2,1)}, bf16[16,4096]{1,0:T(8,128)(2,1)S(1)}, u32[]{:S(2)}, u32[]{:S(2)}) %collective-permute-start.1) | collective-permute-done | bytes 131104 | tf_op jit(solution)/shard_map/ppermute | solution.py:265
  45.2 2.6 %collective-permute-done.2.refs_3_ = bf16[16,4096]{1,0:T(8,128)(2,1)S(1)} collective-permute-done((bf16[16,4096]{1,0:T(8,128)(2,1)}, bf16[16,4096]{1,0:T(8,128)(2,1)S(1)}, u32[]{:S(2)}, u32[]{:S(2)}) %collective-permute-start.2) | collective-permute-done | bytes 131104 | tf_op jit(solution)/shard_map/ppermute | solution.py:265
  47.8 1.0 %collective-permute-start.14 = (bf16[128,768]{1,0:T(8,128)(2,1)}, bf16[128,768]{1,0:T(8,128)(2,1)S(1)}, u32[]{:S(2)}, u32[]{:S(2)}) collective-permute-start(bf16[128,768]{1,0:T(8,128)(2,1)} %hidden.1.hidden_ref.refs_0_), channel_id=1, source_target_pairs={{0,8},{8,0},{16,24},{24,16},{1,9},{9,1},{17,25},{25,17},{2,10},{10... | collective-permute-start | bytes 589832 | tf_op jit(solution)/shard_map/ppermute | solution.py:265
  48.7 4.2 %collective-permute-done.3.refs_4_ = bf16[16,4096]{1,0:T(8,128)(2,1)S(1)} collective-permute-done((bf16[16,4096]{1,0:T(8,128)(2,1)}, bf16[16,4096]{1,0:T(8,128)(2,1)S(1)}, u32[]{:S(2)}, u32[]{:S(2)}) %collective-permute-start.3) | collective-permute-done | bytes 131104 | tf_op jit(solution)/shard_map/ppermute | solution.py:265
  53.6 4.5 %collective-permute-start.16 = (bf16[128,768]{1,0:T(8,128)(2,1)}, bf16[128,768]{1,0:T(8,128)(2,1)S(1)}, u32[]{:S(2)}, u32[]{:S(2)}) collective-permute-start(bf16[128,768]{1,0:T(8,128)(2,1)} %hidden.1.hidden_ref.refs_0_), channel_id=1, source_target_pairs={{0,24},{8,16},{16,8},{24,0},{1,25},{9,17},{17,9},{25,1},{2,26},{10... | collective-permute-start | bytes 589832 | tf_op jit(solution)/shard_map/ppermute | solution.py:265
  58.1 2.1 %collective-permute-start.8 = (bf16[16,4096]{1,0:T(8,128)(2,1)S(1)}, bf16[16,4096]{1,0:T(8,128)(2,1)S(1)}, u32[]{:S(2)}, u32[]{:S(2)}) collective-permute-start(bf16[16,4096]{1,0:T(8,128)(2,1)S(1)} %copy-done.14), channel_id=1, source_target_pairs={{0,2},{1,3},{2,0},{3,1},{4,6},{5,7},{6,4},{7,5},{8,10},{9,11},{10,... | collective-permute-start | bytes 393224 | tf_op jit(solution)/shard_map/ppermute | solution.py:265
  61.1 2.0 %combine.1 = (bf16[128,4096]{1,0:T(8,128)(2,1)}, f32[8,128]{1,0:T(8,128)}) custom-call(s32[8,128]{1,0:T(8,128)S(1)} %bitcast.15, f32[128,128]{1,0:T(8,128)S(1)} %get-tuple-element.25.tie_ref.own_ref, bf16[128,4096]{1,0:T(8,128)(2,1)S(1)} %copy-done.2, bf16[16,4096]{1,0:T(8,128)(2,1)S(1)} %copy-done.6, bf16[16,4096]{1,0:T(8,128)(2,1)S(1)} %collective-permute-done.refs_1_, ...), custom_call_target="tpu_custom_call" | custom-call | tf_op jit(solution)/shard_map/combine/pallas_call | solution.py:221
  63.1 1.3 %collective-permute-done.8.refs_2_ = bf16[16,4096]{1,0:T(8,128)(2,1)S(1)} collective-permute-done((bf16[16,4096]{1,0:T(8,128)(2,1)S(1)}, bf16[16,4096]{1,0:T(8,128)(2,1)S(1)}, u32[]{:S(2)}, u32[]{:S(2)}) %collective-permute-start.8) | collective-permute-done | bytes 131104 | tf_op jit(solution)/shard_map/ppermute | solution.py:265
  64.5 1.9 %collective-permute-done.9.refs_3_ = bf16[16,4096]{1,0:T(8,128)(2,1)S(1)} collective-permute-done((bf16[16,4096]{1,0:T(8,128)(2,1)S(1)}, bf16[16,4096]{1,0:T(8,128)(2,1)S(1)}, u32[]{:S(2)}, u32[]{:S(2)}) %collective-permute-start.9) | collective-permute-done | bytes 131104 | tf_op jit(solution)/shard_map/ppermute | solution.py:265
  66.3 3.0 %expert_backward.1 = bf16[128,1536]{1,0:T(8,128)(2,1)} custom-call(bf16[128,1536]{1,0:T(8,128)(2,1)S(1)} %bitcast.13, bf16[768,4096]{1,0:T(8,128)(2,1)S(1)} %get-tuple-element.36.weight_ref, bf16[16,4096]{1,0:T(8,128)(2,1)S(1)} %copy-done.5, bf16[16,4096]{1,0:T(8,128)(2,1)S(1)} %collective-permute-done.7.refs_1_, ...), custom_call_target="tpu_custom_call" | custom-call | tf_op jit(solution)/shard_map/expert_backward/pallas_call | solution.py:178
  69.8 3.1 %weight_grad.1 = bf16[1024,768]{1,0:T(8,128)(2,1)} custom-call(bf16[512,1024]{1,0:T(8,128)(2,1)S(1)} %bitcast.11, bf16[128,768]{1,0:T(8,128)(2,1)} %hidden.1.hidden_ref.refs_0_, bf16[128,768]{1,0:T(8,128)(2,1)S(1)} %collective-permute-done.14.refs_1_, bf16[128,768]{1,0:T(8,128)(2,1)S(1)} %collective-permute-done.15.refs_2_, ...), custom_call_target="tpu_custom_call" | custom-call | tf_op jit(solution)/shard_map/weight_grad/pallas_call | solution.py:252
  (48 shorter events, 7.2 us)
Async XLA Ops:
  4.5 55.7 %copy-start.2 = (bf16[128,4096]{1,0:T(8,128)(2,1)S(1)}, bf16[128,4096]{1,0:T(8,128)(2,1)}, u32[]{:S(2)}) copy-start(bf16[128,4096]{1,0:T(8,128)(2,1)} %dout_ref.3) | copy-start | bytes 3145732
  4.5 55.7 %copy-start.8 = (s32[128,8]{0,1:T(8,128)S(1)}, s32[128,8]{0,1:T(8,128)}, u32[]{:S(2)}) copy-start(s32[128,8]{0,1:T(8,128)} %param.8) | copy-start | bytes 12292
  4.5 61.8 %copy-start.4 = (bf16[1,1,128,1536]{3,2,1,0:T(8,128)(2,1)S(1)}, bf16[1,1,128,1536]{3,2,1,0:T(8,128)(2,1)}, u32[]{:S(2)}) copy-start(bf16[1,1,128,1536]{3,2,1,0:T(8,128)(2,1)} %param.12) | copy-start | bytes 1179652
  6.9 51.1 %copy-start.14 = (bf16[16,4096]{1,0:T(8,128)(2,1)S(1)}, bf16[16,4096]{1,0:T(8,128)(2,1)}, u32[]{:S(2)}) copy-start(bf16[16,4096]{1,0:T(8,128)(2,1)} %get-tuple-element.39) | copy-start | bytes 393220
  6.9 53.2 %copy-start.13 = (bf16[16,4096]{1,0:T(8,128)(2,1)S(1)}, bf16[16,4096]{1,0:T(8,128)(2,1)}, u32[]{:S(2)}) copy-start(bf16[16,4096]{1,0:T(8,128)(2,1)} %get-tuple-element.40) | copy-start | bytes 393220
  7.0 59.4 %copy-start.5 = (bf16[16,4096]{1,0:T(8,128)(2,1)S(1)}, bf16[16,4096]{1,0:T(8,128)(2,1)}, u32[]{:S(2)}) copy-start(bf16[16,4096]{1,0:T(8,128)(2,1)} %get-tuple-element.37.refs_0_) | copy-start | bytes 393220
  7.0 62.8 %all-to-all-start = ((bf16[32,16,1024]{2,1,0:T(8,128)(2,1)}), bf16[32,16,1024]{2,1,0:T(8,128)(2,1)S(1)}, u32[]{:S(2)}, u32[]{:S(2)}) async-start(bf16[32,16,1024]{2,1,0:T(8,128)(2,1)} %bitcast.19), calls=%async_computation | async-start | bytes 2097152 | tf_op jit(solution)/shard_map/all_to_all | solution.py:278
  14.3 21.6 %collective-permute-start.10 = (bf16[16,4096]{1,0:T(8,128)(2,1)}, bf16[16,4096]{1,0:T(8,128)(2,1)S(1)}, u32[]{:S(2)}, u32[]{:S(2)}) collective-permute-start(bf16[16,4096]{1,0:T(8,128)(2,1)} %get-tuple-element.41), channel_id=1, source_target_pairs={{0,4},{1,5},{2,6},{3,7},{4,0},{5,1},{6,2},{7,3},{8,12},{9,13},{10,... | collective-permute-start | bytes 393224 | tf_op jit(solution)/shard_map/ppermute | solution.py:265
  16.1 22.3 %collective-permute-start.11 = (bf16[16,4096]{1,0:T(8,128)(2,1)}, bf16[16,4096]{1,0:T(8,128)(2,1)S(1)}, u32[]{:S(2)}, u32[]{:S(2)}) collective-permute-start(bf16[16,4096]{1,0:T(8,128)(2,1)} %get-tuple-element.42), channel_id=1, source_target_pairs={{0,5},{1,4},{2,7},{3,6},{4,1},{5,0},{6,3},{7,2},{8,13},{9,12},{10,... | collective-permute-start | bytes 393224 | tf_op jit(solution)/shard_map/ppermute | solution.py:265
  16.1 24.4 %collective-permute-start.12 = (bf16[16,4096]{1,0:T(8,128)(2,1)}, bf16[16,4096]{1,0:T(8,128)(2,1)S(1)}, u32[]{:S(2)}, u32[]{:S(2)}) collective-permute-start(bf16[16,4096]{1,0:T(8,128)(2,1)} %get-tuple-element.43), channel_id=1, source_target_pairs={{0,6},{1,7},{2,4},{3,5},{4,2},{5,3},{6,0},{7,1},{8,14},{9,15},{10,... | collective-permute-start | bytes 393224 | tf_op jit(solution)/shard_map/ppermute | solution.py:265
  18.5 22.3 %collective-permute-start.13 = (bf16[16,4096]{1,0:T(8,128)(2,1)}, bf16[16,4096]{1,0:T(8,128)(2,1)S(1)}, u32[]{:S(2)}, u32[]{:S(2)}) collective-permute-start(bf16[16,4096]{1,0:T(8,128)(2,1)} %get-tuple-element.44), channel_id=1, source_target_pairs={{0,7},{1,6},{2,5},{3,4},{4,3},{5,2},{6,1},{7,0},{8,15},{9,14},{10,... | collective-permute-start | bytes 393224 | tf_op jit(solution)/shard_map/ppermute | solution.py:265
  18.8 22.0 %collective-permute-start.7 = (bf16[16,4096]{1,0:T(8,128)(2,1)}, bf16[16,4096]{1,0:T(8,128)(2,1)S(1)}, u32[]{:S(2)}, u32[]{:S(2)}) collective-permute-start(bf16[16,4096]{1,0:T(8,128)(2,1)} %get-tuple-element.38), channel_id=1, source_target_pairs={{0,1},{1,0},{2,3},{3,2},{4,5},{5,4},{6,7},{7,6},{8,9},{9,8},{10,11... | collective-permute-start | bytes 393224 | tf_op jit(solution)/shard_map/ppermute | solution.py:265
  35.9 6.2 %collective-permute-start = (bf16[16,4096]{1,0:T(8,128)(2,1)}, bf16[16,4096]{1,0:T(8,128)(2,1)S(1)}, u32[]{:S(2)}, u32[]{:S(2)}) collective-permute-start(bf16[16,4096]{1,0:T(8,128)(2,1)} %get-tuple-element.27), channel_id=1, source_target_pairs={{0,1},{1,0},{2,3},{3,2},{4,5},{5,4},{6,7},{7,6},{8,9},{9,8},{10,11... | collective-permute-start | bytes 393224 | tf_op jit(solution)/shard_map/ppermute | solution.py:265
  38.4 6.6 %collective-permute-start.1 = (bf16[16,4096]{1,0:T(8,128)(2,1)}, bf16[16,4096]{1,0:T(8,128)(2,1)S(1)}, u32[]{:S(2)}, u32[]{:S(2)}) collective-permute-start(bf16[16,4096]{1,0:T(8,128)(2,1)} %get-tuple-element.28), channel_id=1, source_target_pairs={{0,2},{1,3},{2,0},{3,1},{4,6},{5,7},{6,4},{7,5},{8,10},{9,11},{10,... | collective-permute-start | bytes 393224 | tf_op jit(solution)/shard_map/ppermute | solution.py:265
  40.5 7.2 %collective-permute-start.2 = (bf16[16,4096]{1,0:T(8,128)(2,1)}, bf16[16,4096]{1,0:T(8,128)(2,1)S(1)}, u32[]{:S(2)}, u32[]{:S(2)}) collective-permute-start(bf16[16,4096]{1,0:T(8,128)(2,1)} %get-tuple-element.29), channel_id=1, source_target_pairs={{0,3},{1,2},{2,1},{3,0},{4,7},{5,6},{6,5},{7,4},{8,11},{9,10},{10,... | collective-permute-start | bytes 393224 | tf_op jit(solution)/shard_map/ppermute | solution.py:265
  40.8 12.2 %collective-permute-start.3 = (bf16[16,4096]{1,0:T(8,128)(2,1)}, bf16[16,4096]{1,0:T(8,128)(2,1)S(1)}, u32[]{:S(2)}, u32[]{:S(2)}) collective-permute-start(bf16[16,4096]{1,0:T(8,128)(2,1)} %get-tuple-element.30), channel_id=1, source_target_pairs={{0,4},{1,5},{2,6},{3,7},{4,0},{5,1},{6,2},{7,3},{8,12},{9,13},{10,... | collective-permute-start | bytes 393224 | tf_op jit(solution)/shard_map/ppermute | solution.py:265
  40.8 12.9 %collective-permute-start.4 = (bf16[16,4096]{1,0:T(8,128)(2,1)}, bf16[16,4096]{1,0:T(8,128)(2,1)S(1)}, u32[]{:S(2)}, u32[]{:S(2)}) collective-permute-start(bf16[16,4096]{1,0:T(8,128)(2,1)} %get-tuple-element.31), channel_id=1, source_target_pairs={{0,5},{1,4},{2,7},{3,6},{4,1},{5,0},{6,3},{7,2},{8,13},{9,12},{10,... | collective-permute-start | bytes 393224 | tf_op jit(solution)/shard_map/ppermute | solution.py:265
  42.0 16.1 %collective-permute-start.5 = (bf16[16,4096]{1,0:T(8,128)(2,1)}, bf16[16,4096]{1,0:T(8,128)(2,1)S(1)}, u32[]{:S(2)}, u32[]{:S(2)}) collective-permute-start(bf16[16,4096]{1,0:T(8,128)(2,1)} %get-tuple-element.32), channel_id=1, source_target_pairs={{0,6},{1,7},{2,4},{3,5},{4,2},{5,3},{6,0},{7,1},{8,14},{9,15},{10,... | collective-permute-start | bytes 393224 | tf_op jit(solution)/shard_map/ppermute | solution.py:265
  45.1 15.1 %collective-permute-start.6 = (bf16[16,4096]{1,0:T(8,128)(2,1)}, bf16[16,4096]{1,0:T(8,128)(2,1)S(1)}, u32[]{:S(2)}, u32[]{:S(2)}) collective-permute-start(bf16[16,4096]{1,0:T(8,128)(2,1)} %get-tuple-element.33), channel_id=1, source_target_pairs={{0,7},{1,6},{2,5},{3,4},{4,3},{5,2},{6,1},{7,0},{8,15},{9,14},{10,... | collective-permute-start | bytes 393224 | tf_op jit(solution)/shard_map/ppermute | solution.py:265
  47.8 21.5 %collective-permute-start.14 = (bf16[128,768]{1,0:T(8,128)(2,1)}, bf16[128,768]{1,0:T(8,128)(2,1)S(1)}, u32[]{:S(2)}, u32[]{:S(2)}) collective-permute-start(bf16[128,768]{1,0:T(8,128)(2,1)} %hidden.1.hidden_ref.refs_0_), channel_id=1, source_target_pairs={{0,8},{8,0},{16,24},{24,16},{1,9},{9,1},{17,25},{25,17},{2,10},{10... | collective-permute-start | bytes 589832 | tf_op jit(solution)/shard_map/ppermute | solution.py:265
  53.0 16.8 %collective-permute-start.15 = (bf16[128,768]{1,0:T(8,128)(2,1)}, bf16[128,768]{1,0:T(8,128)(2,1)S(1)}, u32[]{:S(2)}, u32[]{:S(2)}) collective-permute-start(bf16[128,768]{1,0:T(8,128)(2,1)} %hidden.1.hidden_ref.refs_0_), channel_id=1, source_target_pairs={{0,16},{8,24},{16,0},{24,8},{1,17},{9,25},{17,1},{25,9},{2,18},{10... | collective-permute-start | bytes 589832 | tf_op jit(solution)/shard_map/ppermute | solution.py:265
  53.6 16.1 %collective-permute-start.16 = (bf16[128,768]{1,0:T(8,128)(2,1)}, bf16[128,768]{1,0:T(8,128)(2,1)S(1)}, u32[]{:S(2)}, u32[]{:S(2)}) collective-permute-start(bf16[128,768]{1,0:T(8,128)(2,1)} %hidden.1.hidden_ref.refs_0_), channel_id=1, source_target_pairs={{0,24},{8,16},{16,8},{24,0},{1,25},{9,17},{17,9},{25,1},{2,26},{10... | collective-permute-start | bytes 589832 | tf_op jit(solution)/shard_map/ppermute | solution.py:265
  58.1 6.4 %collective-permute-start.8 = (bf16[16,4096]{1,0:T(8,128)(2,1)S(1)}, bf16[16,4096]{1,0:T(8,128)(2,1)S(1)}, u32[]{:S(2)}, u32[]{:S(2)}) collective-permute-start(bf16[16,4096]{1,0:T(8,128)(2,1)S(1)} %copy-done.14), channel_id=1, source_target_pairs={{0,2},{1,3},{2,0},{3,1},{4,6},{5,7},{6,4},{7,5},{8,10},{9,11},{10,... | collective-permute-start | bytes 393224 | tf_op jit(solution)/shard_map/ppermute | solution.py:265
  60.2 6.1 %collective-permute-start.9 = (bf16[16,4096]{1,0:T(8,128)(2,1)S(1)}, bf16[16,4096]{1,0:T(8,128)(2,1)S(1)}, u32[]{:S(2)}, u32[]{:S(2)}) collective-permute-start(bf16[16,4096]{1,0:T(8,128)(2,1)S(1)} %copy-done.13), channel_id=1, source_target_pairs={{0,3},{1,2},{2,1},{3,0},{4,7},{5,6},{6,5},{7,4},{8,11},{9,10},{10,... | collective-permute-start | bytes 393224 | tf_op jit(solution)/shard_map/ppermute | solution.py:265
  (9 other events, 9.3 us)

commit v3 on v2

v3 whole, which is shorter than its diff:
```python
import functools

import jax
import jax.numpy as jnp
from jax import lax
from jax.experimental import pallas as pl
from jax.experimental.pallas import tpu as pltpu
from jax.sharding import PartitionSpec as P

QB = 128
CAP = 16
VMEM_LIMIT = 40 * 1024 * 1024

bf16 = jnp.bfloat16
f32 = jnp.float32

VMEM = pl.BlockSpec(memory_space=pltpu.VMEM)
ANY = pl.BlockSpec(memory_space=pl.ANY)
HBM = pl.BlockSpec(memory_space=pltpu.HBM)


def params():
    return pltpu.CompilerParams(vmem_limit_bytes=VMEM_LIMIT)


def hbm(value):
    return pltpu.with_memory_space_constraint(value, pltpu.HBM)


def chunks(total, size):
    return [pl.ds(start, size) for start in range(0, total, size)]


def hidden_kernel(gate_up_ref, tie_ref, out_ref, gate_up, sem):
    copy = pltpu.make_async_copy(gate_up_ref, gate_up, sem)
    copy.start()
    copy.wait()
    hid = out_ref.shape[1]
    gate = gate_up[:, :hid].astype(f32)
    up = gate_up[:, hid:].astype(f32)
    out_ref[...] = (gate * jax.nn.sigmoid(gate) * up).astype(bf16)


def make_hidden(gate_up, tie):
    slots, double = gate_up.shape
    return pl.pallas_call(
        hidden_kernel,
        out_shape=pltpu.HBM((slots, double // 2), bf16),
        in_specs=[HBM, ANY],
        out_specs=VMEM,
        scratch_shapes=[pltpu.VMEM((slots, double), bf16), pltpu.SemaphoreType.DMA],
        compiler_params=params(),
        name="hidden",
    )(hbm(gate_up), tie)


def dispatch_kernel(
    flight, groups, cap_hbm, hot_hbm, ids_hbm, probs_hbm, dout_hbm, own_ref, rows_hbm,
    cap_ref, hot_ref, ids_ref, probs_ref, dout, rows, small_sems, in_sems, out_sems
):
    topk, tokens = ids_ref.shape
    slots = flight * CAP
    group = lax.axis_index("dp")
    share = dout_hbm.shape[1] // groups
    small = [
        pltpu.make_async_copy(src, dst, small_sems.at[i])
        for i, (src, dst) in enumerate(
            [(ids_hbm, ids_ref), (probs_hbm, probs_ref), (cap_hbm, cap_ref), (hot_hbm, hot_ref)]
        )
    ]
    loads = [
        pltpu.make_async_copy(
            dout_hbm.at[:, pl.ds(pl.multiple_of((group ^ j) * share, share), share)],
            dout.at[j],
            in_sems.at[j],
        )
        for j in range(groups)
    ]
    for copy in small + loads:
        copy.start()
    for copy in small:
        copy.wait()
    row = lax.broadcasted_iota(jnp.int32, (slots, 1), 0)
    row_expert = row // CAP
    row_rank = (row % CAP).astype(f32)
    limit = jnp.zeros((slots, 1), jnp.int32)
    for e in range(flight):
        hot = hot_ref[0, 0] == e
        for h in range(1, hot_ref.shape[1]):
            hot = jnp.logical_or(hot, hot_ref[0, h] == e)
        limit = jnp.where(row_expert == e, jnp.where(hot, CAP, cap_ref[e]), limit)
    limit = limit.astype(f32)
    named = jnp.zeros((slots, tokens), f32)
    weight = jnp.zeros((slots, tokens), f32)
    for k in range(topk):
        hit = ids_ref[k : k + 1, :] == row_expert
        named = jnp.where(hit, 1.0, named)
        weight = jnp.where(hit, probs_ref[k : k + 1, :], weight)
    first = lax.broadcasted_iota(jnp.int32, (tokens, tokens), 0)
    second = lax.broadcasted_iota(jnp.int32, (tokens, tokens), 1)
    before = (first < second).astype(f32).astype(bf16)
    rank = jnp.dot(named.astype(bf16), before, preferred_element_type=f32)
    owns = (named > 0.0) & (rank == row_rank) & (rank < limit)
    own_weight = jnp.where(owns, weight, 0.0)
    own_ref[...] = own_weight
    owner = jnp.where(owns, 1.0, 0.0).astype(bf16)
    slot_weight = jnp.sum(own_weight, axis=1, keepdims=True)
    stores = []
    for j in range(groups):
        loads[j].wait()
        part = jnp.dot(owner, dout[j], preferred_element_type=f32)
        rows[j] = (part * slot_weight).astype(bf16).reshape(flight, CAP, share)
        stores.append(pltpu.make_async_copy(rows.at[j], rows_hbm.at[:, j], out_sems.at[j]))
        stores[j].start()
    for copy in stores:
        copy.wait()


def dispatch(capacity, hot_row, ids, probs, d_out, flight, groups):
    tokens, width = d_out.shape
    slots = flight * CAP
    share = width // groups
    return pl.pallas_call(
        functools.partial(dispatch_kernel, flight, groups),
        out_shape=(
            jax.ShapeDtypeStruct((slots, tokens), f32),
            pltpu.HBM((flight, groups, CAP, share), bf16),
        ),
        in_specs=[HBM] * 5,
        out_specs=(VMEM, HBM),
        scratch_shapes=[
            pltpu.SMEM(capacity.shape, jnp.int32),
            pltpu.SMEM(hot_row.shape, jnp.int32),
            pltpu.VMEM(ids.shape, jnp.int32),
            pltpu.VMEM(probs.shape, f32),
            pltpu.VMEM((groups, tokens, share), bf16),
            pltpu.VMEM((groups, flight, CAP, share), bf16),
            pltpu.SemaphoreType.DMA((4,)),
            pltpu.SemaphoreType.DMA((groups,)),
            pltpu.SemaphoreType.DMA((groups,)),
        ],
        compiler_params=params(),
        name="dispatch",
    )(hbm(capacity), hbm(hot_row), hbm(ids), hbm(probs), hbm(d_out))


def forward_kernel(
    flight, block, scale_hbm, hidden_hbm, quant_hbm, weight_ref, out_hbm,
    scale_ref, hidden, quant, out, small_sems, in_sems, out_sems
):
    hid, width = quant.shape
    steps = chunks(width, block)
    small = [
        pltpu.make_async_copy(scale_hbm, scale_ref, small_sems.at[0]),
        pltpu.make_async_copy(hidden_hbm, hidden, small_sems.at[1]),
    ]
    loads = [
        pltpu.make_async_copy(quant_hbm.at[:, cols], quant.at[:, cols], in_sems.at[c])
        for c, cols in enumerate(steps)
    ]
    for copy in small + loads:
        copy.start()
    for copy in small:
        copy.wait()
    stores = []
    for c, cols in enumerate(steps):
        loads[c].wait()
        for i in range(hid // QB):
            for j in range(block // QB):
                at = (pl.ds(i * QB, QB), pl.ds(c * block + j * QB, QB))
                scale = scale_ref[i, 0, c * (block // QB) + j]
                weight_ref[at] = (quant[at].astype(f32) * scale).astype(bf16)
        part = jnp.dot(hidden[...], weight_ref[:, cols], preferred_element_type=f32)
        out[:, :, cols] = part.astype(bf16).reshape(flight, CAP, block)
        stores.append(
            pltpu.make_async_copy(out.at[:, :, cols], out_hbm.at[:, :, cols], out_sems.at[c])
        )
        stores[c].start()
    for copy in stores:
        copy.wait()


def forward(scale, hidden, quant, flight, block=512):
    hid, width = quant.shape
    return pl.pallas_call(
        functools.partial(forward_kernel, flight, block),
        out_shape=(
            jax.ShapeDtypeStruct((hid, width), bf16),
            pltpu.HBM((flight, CAP, width), bf16),
        ),
        in_specs=[HBM, HBM, HBM],
        out_specs=(VMEM, HBM),
        scratch_shapes=[
            pltpu.SMEM(scale.shape, f32),
            pltpu.VMEM(hidden.shape, bf16),
            pltpu.VMEM((hid, width), bf16),
            pltpu.VMEM((flight, CAP, width), bf16),
            pltpu.SemaphoreType.DMA((2,)),
            pltpu.SemaphoreType.DMA((width // block,)),
            pltpu.SemaphoreType.DMA((width // block,)),
        ],
        compiler_params=params(),
        name="expert_forward",
    )(hbm(scale), hbm(hidden), hbm(quant))


def split_kernel(groups, rows_ref, tie_ref, *refs):
    outs, sems = refs[:-1], refs[-1]
    copies = [
        pltpu.make_async_copy(rows_ref.at[:, j], outs[j - 1], sems.at[j - 1])
        for j in range(1, groups)
    ]
    for copy in copies:
        copy.start()
    for copy in copies:
        copy.wait()


def split(rows, tie):
    flight, groups, cap, share = rows.shape
    return pl.pallas_call(
        functools.partial(split_kernel, groups),
        out_shape=(pltpu.HBM((flight, cap, share), bf16),) * (groups - 1),
        in_specs=[ANY, ANY],
        out_specs=(HBM,) * (groups - 1),
        scratch_shapes=[pltpu.SemaphoreType.DMA((groups - 1,))],
        compiler_params=params(),
        name="split",
    )(rows, hbm(tie))


def backward_kernel(gate_up_hbm, weight_ref, rows_ref, tie_ref, out_ref, gate_up, acc, sem):
    copy = pltpu.make_async_copy(gate_up_hbm, gate_up, sem)
    copy.start()
    hid = weight_ref.shape[0]
    flight, groups, cap, share = rows_ref.shape
    group = lax.axis_index("dp")
    for j in range(groups):
        cols = pl.ds(pl.multiple_of((group ^ j) * share, share), share)
        part = lax.dot_general(
            rows_ref[:, j].reshape(flight * cap, share),
            weight_ref[:, cols],
            (((1,), (1,)), ((), ())),
            preferred_element_type=f32,
        )
        if j == 0:
            acc[...] = part
        else:
            acc[...] += part
    copy.wait()
    gate = gate_up[:, :hid].astype(f32)
    up = gate_up[:, hid:].astype(f32)
    sig = jax.nn.sigmoid(gate)
    d_hidden = acc[...]
    out_ref[:, :hid] = (d_hidden * up * sig * (1.0 + gate * (1.0 - sig))).astype(bf16)
    out_ref[:, hid:] = (d_hidden * (gate * sig)).astype(bf16)


def backward(gate_up, weight, rows, tie):
    slots, double = gate_up.shape
    hid = weight.shape[0]
    return pl.pallas_call(
        backward_kernel,
        out_shape=jax.ShapeDtypeStruct((slots, double), bf16),
        in_specs=[HBM, VMEM, VMEM, ANY],
        out_specs=VMEM,
        scratch_shapes=[
            pltpu.VMEM((slots, double), bf16),
            pltpu.VMEM((slots, hid), f32),
            pltpu.SemaphoreType.DMA,
        ],
        compiler_params=params(),
        name="expert_backward",
    )(hbm(gate_up), weight, rows, hbm(tie))


def combine_kernel(
    block, ids_hbm, own_ref, dout_hbm, ret_ref, out_ref, dprobs_ref, ids_ref, dout, sems
):
    copies = [
        pltpu.make_async_copy(ids_hbm, ids_ref, sems.at[0]),
        pltpu.make_async_copy(dout_hbm, dout, sems.at[1]),
    ]
    for copy in copies:
        copy.start()
    topk, tokens = ids_ref.shape
    slots = own_ref.shape[0]
    width = dout.shape[1]
    own = own_ref[...]
    turned = own.T
    high = turned.astype(bf16)
    low = (turned - high.astype(f32)).astype(bf16)
    total = jnp.zeros((slots, tokens), f32)
    for copy in copies:
        copy.wait()
    for cols in chunks(width, block):
        here = ret_ref[:, :, cols].reshape(slots, block)
        out = jnp.dot(high, here, preferred_element_type=f32)
        out = out + jnp.dot(low, here, preferred_element_type=f32)
        out_ref[:, cols] = out.astype(bf16)
        total = total + lax.dot_general(
            here, dout[:, cols], (((1,), (1,)), ((), ())), preferred_element_type=f32
        )
    inner = jnp.where(own > 0.0, total, 0.0)
    row_expert = lax.broadcasted_iota(jnp.int32, (slots, 1), 0) // CAP
    for k in range(topk):
        mine = jnp.where(ids_ref[k : k + 1, :] == row_expert, inner, 0.0)
        dprobs_ref[k : k + 1, :] = jnp.sum(mine, axis=0, keepdims=True)


def combine(ids, own, d_out, returned, block=1024):
    tokens, width = d_out.shape
    return pl.pallas_call(
        functools.partial(combine_kernel, block),
        out_shape=(
            jax.ShapeDtypeStruct((tokens, width), bf16),
            jax.ShapeDtypeStruct(ids.shape, f32),
        ),
        in_specs=[HBM, VMEM, HBM, VMEM],
        out_specs=(VMEM, VMEM),
        scratch_shapes=[
            pltpu.VMEM(ids.shape, jnp.int32),
            pltpu.VMEM((tokens, width), bf16),
            pltpu.SemaphoreType.DMA((2,)),
        ],
        compiler_params=params(),
        name="combine",
    )(hbm(ids), own, hbm(d_out), returned)


def weight_grad_kernel(groups, block, rows_ref, *refs):
    part_refs, hid_refs = refs[: groups - 1], refs[groups - 1 : 2 * groups - 1]
    out_hbm, grads, hidden, out, sems, out_sems = refs[2 * groups - 1 :]
    flight, cap, share = part_refs[0].shape
    slots = flight * cap
    copies = []
    for j in range(groups):
        src = rows_ref.at[:, 0] if j == 0 else part_refs[j - 1]
        copies.append(
            pltpu.make_async_copy(src, grads.at[pl.ds(j * flight, flight)], sems.at[2 * j])
        )
        copies.append(
            pltpu.make_async_copy(
                hid_refs[j], hidden.at[pl.ds(j * slots, slots)], sems.at[2 * j + 1]
            )
        )
    for copy in copies:
        copy.start()
    for copy in copies:
        copy.wait()
    stores = []
    for c, cols in enumerate(chunks(share, block)):
        out[cols, :] = lax.dot_general(
            grads[:, :, cols].reshape(groups * slots, block),
            hidden[...],
            (((0,), (0,)), ((), ())),
            preferred_element_type=f32,
        ).astype(bf16)
        stores.append(pltpu.make_async_copy(out.at[cols], out_hbm.at[cols], out_sems.at[c]))
        stores[c].start()
    for copy in stores:
        copy.wait()


def weight_grad(rows, parts, hiddens, block=256):
    flight, groups, cap, share = rows.shape
    slots, hid = hiddens[0].shape
    return pl.pallas_call(
        functools.partial(weight_grad_kernel, groups, block),
        out_shape=pltpu.HBM((share, hid), bf16),
        in_specs=[ANY] * (2 * groups),
        out_specs=HBM,
        scratch_shapes=[
            pltpu.VMEM((groups * flight, cap, share), bf16),
            pltpu.VMEM((groups * slots, hid), bf16),
            pltpu.VMEM((share, hid), bf16),
            pltpu.SemaphoreType.DMA((2 * groups,)),
            pltpu.SemaphoreType.DMA((share // block,)),
        ],
        compiler_params=params(),
        name="weight_grad",
    )(rows, *parts, hbm(hiddens[0]), *hiddens[1:])


def swap(value, axis, j):
    size = lax.axis_size(axis)
    return lax.ppermute(value, axis, [(i, i ^ j) for i in range(size)])


def exchange(value):
    return lax.all_to_all(value, "expert", split_axis=0, concat_axis=0, tiled=True)


def shards(route_ids, route_probs, capacity, hot_lists, gate_up, w_quant, w_scale, d_out):
    flight = lax.axis_size("expert")
    groups = lax.axis_size("dp")
    gate_up = gate_up[0, 0]
    ids, probs = route_ids.T, route_probs.T
    own, rows = dispatch(capacity, hot_lists, ids, probs, d_out, flight, groups)
    arrived = exchange(rows)
    hidden = make_hidden(gate_up, own)
    hiddens = [hidden] + [swap(hidden, "dp", j) for j in range(1, groups)]
    weight, expert_out = forward(w_scale.transpose(1, 0, 2), hidden, w_quant[0], flight)
    returned = exchange(expert_out)
    pieces = split(arrived, expert_out)
    parts = [swap(pieces[j - 1], "dp", j) for j in range(1, groups)]
    d_gate_up = backward(gate_up, weight, arrived, pieces[0])
    combined, d_probs = combine(ids, own, d_out, returned)
    d_weight = weight_grad(arrived, parts, hiddens)
    return (combined, d_probs.T, d_gate_up[None, None], d_weight[None])


def solution(mesh):
    placed = (
        P(("dp", "expert"), None),
        P(("dp", "expert"), None),
        P(),
        P("dp", None),
        P("dp", "expert", None, None),
        P("expert", None, None),
        P("expert", None, None),
        P(("dp", "expert"), None),
    )
    return jax.shard_map(
        shards,
        mesh=mesh,
        in_specs=placed,
        out_specs=(
            P(("dp", "expert"), None),
            P(("dp", "expert"), None),
            P("dp", "expert", None, None),
            P("expert", "dp", None),
        ),
        check_vma=False,
    )
```

time: 73.4 us -> 75.6 us (1.030)
  the two profiles are of different devices: /device:TPU:0 before, /device:TPU:18 now
where the time goes in v3:
time: 75.6 us; the launch traced here: 75.2 us
  waiting for transfers between devices  31 us (41%)
  Pallas kernels  22.5 us (30%)
  starting transfers between devices  15.6 us (21%)
  local copies, waits for them, and re-layouts  5.43 us (7%)
    ppermute x6, waiting for transfers between devices, swap(): return lax.ppermute(value, axis, [(i, i ^ j) for i in range(size)])  26.7 us
    all_to_all x2, starting transfers between devices, exchange(): lax.all_to_all(value, 'expert', split_axis=0, concat_axis=0, tiled=True)  9.24 us
    pallas_call x1, Pallas kernels, forward(): pl.pallas_call(functools.partial(forward_kernel, flight, block), out_shap...  7.02 us
    ppermute x6, starting transfers between devices, swap(): return lax.ppermute(value, axis, [(i, i ^ j) for i in range(size)])  6.37 us
    unnamed x4, local copies, waits for them, and re-layouts  5.43 us
    all_to_all x2, waiting for transfers between devices, exchange(): lax.all_to_all(value, 'expert', split_axis=0, concat_axis=0, tiled=True)  4.3 us
    pallas_call x1, Pallas kernels, backward(): pl.pallas_call(backward_kernel, out_shape=jax.ShapeDtypeStruct((slots, do...  3.93 us
    pallas_call x1, Pallas kernels, combine(): pl.pallas_call(functools.partial(combine_kernel, block), out_shape=(jax.S...  3.24 us
  transfers between devices with their start and end apart: 8, of which 5 were waited for; matrix products, arithmetic and copies ran while one was open for 0% of the time, Pallas kernels for 22%

profile of v3, /device:TPU:18, one launch (start us, length us, event | category | flops | bytes accessed | tf_op | source)
XLA Modules:
  0.0 75.2 jit_solution(5487052752382146951)
XLA Ops:
  0.6 2.8 %dispatch.1 = (f32[128,128]{1,0:T(8,128)S(1)}, bf16[8,4,16,1024]{3,2,1,0:T(8,128)(2,1)}) custom-call(s32[8]{0:T(128)} %cap_hbm.1, s32[1,4]{1,0:T(1,128)} %hot_hbm.1, s32[8,128]{1,0:T(8,128)} %bitcast.13, f32[8,128]{1,0:T(8,128)} %bitcast.15, bf16[128,4096]{1,0:T(8,128)(2,1)} %dout_hbm.3), custom_call_target="tpu_custom_call" | custom-call | tf_op jit(solution)/shard_map/dispatch/pallas_call | solution.py:123
  3.4 4.3 %all-to-all-start.1 = ((bf16[8,4,16,1024]{3,2,1,0:T(8,128)(2,1)}), bf16[8,4,16,1024]{3,2,1,0:T(8,128)(2,1)S(1)}, u32[]{:S(2)}, u32[]{:S(2)}) async-start(bf16[8,4,16,1024]{3,2,1,0:T(8,128)(2,1)} %get-tuple-element.18), calls=%async_computation.1 | async-start | bytes 2097152 | tf_op jit(solution)/shard_map/all_to_all | solution.py:391
  7.7 1.8 %hidden.1.hidden_hbm.refs_3_ = bf16[128,768]{1,0:T(8,128)(2,1)} custom-call(bf16[128,1536]{1,0:T(8,128)(2,1)} %bitcast.9, f32[128,128]{1,0:T(8,128)S(1)} %get-tuple-element.13.tie_ref.own_ref), custom_call_target="tpu_custom_call" | custom-call | tf_op jit(solution)/shard_map/hidden/pallas_call | solution.py:46
  9.5 7.0 %expert_forward.1 = (bf16[768,4096]{1,0:T(8,128)(2,1)S(1)}, bf16[8,16,4096]{2,1,0:T(8,128)(2,1)}) custom-call(f32[6,1,32]{2,1,0:T(1,128)} %bitcast.16, bf16[128,768]{1,0:T(8,128)(2,1)} %hidden.1.hidden_hbm.refs_3_, bf16[768,4096]{1,0:T(8,128)(2,1)} %bitcast.8), custom_call_target="tpu_custom_call" | custom-call | tf_op jit(solution)/shard_map/expert_forward/pallas_call | solution.py:185
  16.5 2.6 %copy-done = bf16[768,4096]{1,0:T(8,128)(2,1)} copy-done((bf16[768,4096]{1,0:T(8,128)(2,1)}, bf16[768,4096]{1,0:T(8,128)(2,1)S(1)}, u32[]{:S(2)}) %copy-start) | copy-done | bytes 6291480
  19.1 2.4 %all-to-all-done.1.rows_ref = bf16[8,4,16,1024]{3,2,1,0:T(8,128)(2,1)S(1)} async-done(((bf16[8,4,16,1024]{3,2,1,0:T(8,128)(2,1)}), bf16[8,4,16,1024]{3,2,1,0:T(8,128)(2,1)S(1)}, u32[]{:S(2)}, u32[]{:S(2)}) %all-to-all-start.1) | async-done | bytes 1048608 | tf_op jit(solution)/shard_map/all_to_all | solution.py:391
  21.6 5.0 %all-to-all-start = ((bf16[8,16,4096]{2,1,0:T(8,128)(2,1)}), bf16[8,16,4096]{2,1,0:T(8,128)(2,1)S(1)}, u32[]{:S(2)}, u32[]{:S(2)}) async-start(bf16[8,16,4096]{2,1,0:T(8,128)(2,1)} %get-tuple-element.14.tie_ref), calls=%async_computation | async-start | bytes 2097152 | tf_op jit(solution)/shard_map/all_to_all | solution.py:391
  26.6 1.6 %collective-permute-start.3 = (bf16[128,768]{1,0:T(8,128)(2,1)}, bf16[128,768]{1,0:T(8,128)(2,1)S(1)}, u32[]{:S(2)}, u32[]{:S(2)}) collective-permute-start(bf16[128,768]{1,0:T(8,128)(2,1)} %hidden.1.hidden_hbm.refs_3_), channel_id=1, source_target_pairs={{0,8},{8,0},{16,24},{24,16},{1,9},{9,1},{17,25},{25,17},{2,10},{10... | collective-permute-start | bytes 589832 | tf_op jit(solution)/shard_map/ppermute | solution.py:387
  28.1 0.9 %split.1 = (bf16[8,16,1024]{2,1,0:T(8,128)(2,1)}, bf16[8,16,1024]{2,1,0:T(8,128)(2,1)}, bf16[8,16,1024]{2,1,0:T(8,128)(2,1)}) custom-call(bf16[8,4,16,1024]{3,2,1,0:T(8,128)(2,1)S(1)} %all-to-all-done.1.rows_ref, bf16[8,16,4096]{2,1,0:T(8,128)(2,1)} %get-tuple-element.14.tie_ref), custom_call_target="tpu_custom_call" | custom-call | tf_op jit(solution)/shard_map/split/pallas_call | solution.py:221
  29.1 0.5 collective-permute-start
  29.6 0.3 collective-permute-start.1
  29.9 2.7 %collective-permute-start.2 = (bf16[8,16,1024]{2,1,0:T(8,128)(2,1)}, bf16[8,16,1024]{2,1,0:T(8,128)(2,1)S(1)}, u32[]{:S(2)}, u32[]{:S(2)}) collective-permute-start(bf16[8,16,1024]{2,1,0:T(8,128)(2,1)} %get-tuple-element.21), channel_id=1, source_target_pairs={{0,24},{8,16},{16,8},{24,0},{1,25},{9,17},{17,9},{25,1},{2,26},{10... | collective-permute-start | bytes 786440 | tf_op jit(solution)/shard_map/ppermute | solution.py:387
  32.6 1.2 %collective-permute-start.4 = (bf16[128,768]{1,0:T(8,128)(2,1)}, bf16[128,768]{1,0:T(8,128)(2,1)S(1)}, u32[]{:S(2)}, u32[]{:S(2)}) collective-permute-start(bf16[128,768]{1,0:T(8,128)(2,1)} %hidden.1.hidden_hbm.refs_3_), channel_id=1, source_target_pairs={{0,16},{8,24},{16,0},{24,8},{1,17},{9,25},{17,1},{25,9},{2,18},{10... | collective-permute-start | bytes 589832 | tf_op jit(solution)/shard_map/ppermute | solution.py:387
  33.9 4.7 %collective-permute-done.3.refs_4_ = bf16[128,768]{1,0:T(8,128)(2,1)S(1)} collective-permute-done((bf16[128,768]{1,0:T(8,128)(2,1)}, bf16[128,768]{1,0:T(8,128)(2,1)S(1)}, u32[]{:S(2)}, u32[]{:S(2)}) %collective-permute-start.3) | collective-permute-done | bytes 196640 | tf_op jit(solution)/shard_map/ppermute | solution.py:387
  38.6 0.0 collective-permute-start.5
  38.6 1.9 %all-to-all-done.ret_ref = bf16[8,16,4096]{2,1,0:T(8,128)(2,1)S(1)} async-done(((bf16[8,16,4096]{2,1,0:T(8,128)(2,1)}), bf16[8,16,4096]{2,1,0:T(8,128)(2,1)S(1)}, u32[]{:S(2)}, u32[]{:S(2)}) %all-to-all-start) | async-done | bytes 1048608 | tf_op jit(solution)/shard_map/all_to_all | solution.py:391
  40.5 3.2 %combine.1 = (bf16[128,4096]{1,0:T(8,128)(2,1)}, f32[8,128]{1,0:T(8,128)}) custom-call(s32[8,128]{1,0:T(8,128)} %bitcast.14, f32[128,128]{1,0:T(8,128)S(1)} %get-tuple-element.13.tie_ref.own_ref, bf16[128,4096]{1,0:T(8,128)(2,1)} %dout_hbm.3, bf16[8,16,4096]{2,1,0:T(8,128)(2,1)S(1)} %all-to-all-done.ret_ref), custom_call_target="tpu_custom_call" | custom-call | tf_op jit(solution)/shard_map/combine/pallas_call | solution.py:313
  43.7 2.8 %copy-done.1 = bf16[768,4096]{1,0:T(8,128)(2,1)S(1)} copy-done((bf16[768,4096]{1,0:T(8,128)(2,1)S(1)}, bf16[768,4096]{1,0:T(8,128)(2,1)}, u32[]{:S(2)}) %copy-start.1) | copy-done | bytes 6291480
  46.5 3.9 %expert_backward.1 = bf16[128,1536]{1,0:T(8,128)(2,1)} custom-call(bf16[128,1536]{1,0:T(8,128)(2,1)} %bitcast.10, bf16[768,4096]{1,0:T(8,128)(2,1)S(1)} %copy-done.1, bf16[8,4,16,1024]{3,2,1,0:T(8,128)(2,1)S(1)} %all-to-all-done.1.rows_ref, bf16[8,16,1024]{2,1,0:T(8,128)(2,1)} %get-tuple-element.19.tie_ref), custom_call_target="tpu_custom_call" | custom-call | tf_op jit(solution)/shard_map/expert_backward/pallas_call | solution.py:262
  50.5 16.0 %collective-permute-done.4.refs_5_ = bf16[128,768]{1,0:T(8,128)(2,1)S(1)} collective-permute-done((bf16[128,768]{1,0:T(8,128)(2,1)}, bf16[128,768]{1,0:T(8,128)(2,1)S(1)}, u32[]{:S(2)}, u32[]{:S(2)}) %collective-permute-start.4) | collective-permute-done | bytes 196640 | tf_op jit(solution)/shard_map/ppermute | solution.py:387
  66.5 5.9 %collective-permute-done.5.refs_6_ = bf16[128,768]{1,0:T(8,128)(2,1)S(1)} collective-permute-done((bf16[128,768]{1,0:T(8,128)(2,1)}, bf16[128,768]{1,0:T(8,128)(2,1)S(1)}, u32[]{:S(2)}, u32[]{:S(2)}) %collective-permute-start.5) | collective-permute-done | bytes 196640 | tf_op jit(solution)/shard_map/ppermute | solution.py:387
  72.4 0.0 collective-permute-done.refs_0_
  72.4 0.0 collective-permute-done.1.refs_1_
  72.4 2.8 %weight_grad.1 = bf16[1024,768]{1,0:T(8,128)(2,1)} custom-call(bf16[8,4,16,1024]{3,2,1,0:T(8,128)(2,1)S(1)} %all-to-all-done.1.rows_ref, bf16[8,16,1024]{2,1,0:T(8,128)(2,1)S(1)} %collective-permute-done.refs_0_, bf16[8,16,1024]{2,1,0:T(8,128)(2,1)S(1)} %collective-permute-done.1.refs_1_, bf16[8,16,1024]{2,1,0:T(8,128)(2,1)S(1)} %collective-permute-done.2.refs_2_, ...), custom_call_target="tpu_custom_call" | custom-call | tf_op jit(solution)/shard_map/weight_grad/pallas_call | solution.py:368
  (3 shorter events, 0.0 us)
Async XLA Ops:
  3.4 18.2 %all-to-all-start.1 = ((bf16[8,4,16,1024]{3,2,1,0:T(8,128)(2,1)}), bf16[8,4,16,1024]{3,2,1,0:T(8,128)(2,1)S(1)}, u32[]{:S(2)}, u32[]{:S(2)}) async-start(bf16[8,4,16,1024]{3,2,1,0:T(8,128)(2,1)} %get-tuple-element.18), calls=%async_computation.1 | async-start | bytes 2097152 | tf_op jit(solution)/shard_map/all_to_all | solution.py:391
  16.5 2.7 %copy-start = (bf16[768,4096]{1,0:T(8,128)(2,1)}, bf16[768,4096]{1,0:T(8,128)(2,1)S(1)}, u32[]{:S(2)}) copy-start(bf16[768,4096]{1,0:T(8,128)(2,1)S(1)} %get-tuple-element.17.weight_ref) | copy-start | bytes 18874372
  21.6 18.9 %all-to-all-start = ((bf16[8,16,4096]{2,1,0:T(8,128)(2,1)}), bf16[8,16,4096]{2,1,0:T(8,128)(2,1)S(1)}, u32[]{:S(2)}, u32[]{:S(2)}) async-start(bf16[8,16,4096]{2,1,0:T(8,128)(2,1)} %get-tuple-element.14.tie_ref), calls=%async_computation | async-start | bytes 2097152 | tf_op jit(solution)/shard_map/all_to_all | solution.py:391
  26.6 12.1 %collective-permute-start.3 = (bf16[128,768]{1,0:T(8,128)(2,1)}, bf16[128,768]{1,0:T(8,128)(2,1)S(1)}, u32[]{:S(2)}, u32[]{:S(2)}) collective-permute-start(bf16[128,768]{1,0:T(8,128)(2,1)} %hidden.1.hidden_hbm.refs_3_), channel_id=1, source_target_pairs={{0,8},{8,0},{16,24},{24,16},{1,9},{9,1},{17,25},{25,17},{2,10},{10... | collective-permute-start | bytes 589832 | tf_op jit(solution)/shard_map/ppermute | solution.py:387
  29.1 43.3 %collective-permute-start = (bf16[8,16,1024]{2,1,0:T(8,128)(2,1)}, bf16[8,16,1024]{2,1,0:T(8,128)(2,1)S(1)}, u32[]{:S(2)}, u32[]{:S(2)}) collective-permute-start(bf16[8,16,1024]{2,1,0:T(8,128)(2,1)} %get-tuple-element.19.tie_ref), channel_id=1, source_target_pairs={{0,8},{8,0},{16,24},{24,16},{1,9},{9,1},{17,25},{25,17},{2,10},{10... | collective-permute-start | bytes 786440 | tf_op jit(solution)/shard_map/ppermute | solution.py:387
  29.6 42.8 %collective-permute-start.1 = (bf16[8,16,1024]{2,1,0:T(8,128)(2,1)}, bf16[8,16,1024]{2,1,0:T(8,128)(2,1)S(1)}, u32[]{:S(2)}, u32[]{:S(2)}) collective-permute-start(bf16[8,16,1024]{2,1,0:T(8,128)(2,1)} %get-tuple-element.20), channel_id=1, source_target_pairs={{0,16},{8,24},{16,0},{24,8},{1,17},{9,25},{17,1},{25,9},{2,18},{10... | collective-permute-start | bytes 786440 | tf_op jit(solution)/shard_map/ppermute | solution.py:387
  29.9 42.5 %collective-permute-start.2 = (bf16[8,16,1024]{2,1,0:T(8,128)(2,1)}, bf16[8,16,1024]{2,1,0:T(8,128)(2,1)S(1)}, u32[]{:S(2)}, u32[]{:S(2)}) collective-permute-start(bf16[8,16,1024]{2,1,0:T(8,128)(2,1)} %get-tuple-element.21), channel_id=1, source_target_pairs={{0,24},{8,16},{16,8},{24,0},{1,25},{9,17},{17,9},{25,1},{2,26},{10... | collective-permute-start | bytes 786440 | tf_op jit(solution)/shard_map/ppermute | solution.py:387
  32.6 33.8 %collective-permute-start.4 = (bf16[128,768]{1,0:T(8,128)(2,1)}, bf16[128,768]{1,0:T(8,128)(2,1)S(1)}, u32[]{:S(2)}, u32[]{:S(2)}) collective-permute-start(bf16[128,768]{1,0:T(8,128)(2,1)} %hidden.1.hidden_hbm.refs_3_), channel_id=1, source_target_pairs={{0,16},{8,24},{16,0},{24,8},{1,17},{9,25},{17,1},{25,9},{2,18},{10... | collective-permute-start | bytes 589832 | tf_op jit(solution)/shard_map/ppermute | solution.py:387
  38.6 33.8 %collective-permute-start.5 = (bf16[128,768]{1,0:T(8,128)(2,1)}, bf16[128,768]{1,0:T(8,128)(2,1)S(1)}, u32[]{:S(2)}, u32[]{:S(2)}) collective-permute-start(bf16[128,768]{1,0:T(8,128)(2,1)} %hidden.1.hidden_hbm.refs_3_), channel_id=1, source_target_pairs={{0,24},{8,16},{16,8},{24,0},{1,25},{9,17},{17,9},{25,1},{2,26},{10... | collective-permute-start | bytes 589832 | tf_op jit(solution)/shard_map/ppermute | solution.py:387
  43.7 2.8 %copy-start.1 = (bf16[768,4096]{1,0:T(8,128)(2,1)S(1)}, bf16[768,4096]{1,0:T(8,128)(2,1)}, u32[]{:S(2)}) copy-start(bf16[768,4096]{1,0:T(8,128)(2,1)} %copy-done) | copy-start | bytes 18874372
